TPU v7x, 256 devices: a whole 4x4x8 slice. The times are simulated.
256 devices in a mesh: dp: 32 (over x, z_lo, y), tensor: 8 (over z_hi, core).
Axes of the slice: x: 4, y: 4, z: 8 (z_hi: 4, z_lo: 2; z = z_hi * 2 + z_lo), core: 2. Of those that a mesh axis runs over, the one named last changes fastest.
Arguments:
- enc_states: bfloat16 [4096, 8192], P('dp'), may hold values from -170 to 170
- kv_cotangent: bfloat16 [4096, 2048], P('dp', 'tensor'), may hold values from -120 to 120
- out_cotangent: bfloat16 [4096, 8192], P('dp'), may hold values from -400 to 400
- attn_context: bfloat16 [4096, 4096], P('dp', 'tensor'), may hold values from -35 to 35
- next_states: bfloat16 [4096, 8192], P('dp'), may hold values from -6 to 6
- next_context: bfloat16 [4096, 4096], P('dp', 'tensor'), may hold values from -6 to 6
- kv_master: float32 [8192, 2048], P('dp', 'tensor'), may hold values from -0.0625 to 0.0625
- kv_first: float32 [8192, 2048], P('dp', 'tensor'), may hold values from -0.6 to 0.6
- kv_second: float32 [8192, 2048], P('dp', 'tensor'), may hold values from 0.01 to 0.2
- out_master: float32 [8192, 4096], P('dp', 'tensor'), may hold values from -0.09375 to 0.09375
- out_first: float32 [8192, 4096], P('dp', 'tensor'), may hold values from -0.6 to 0.6
- out_second: float32 [8192, 4096], P('dp', 'tensor'), may hold values from 0.01 to 0.2
Outputs:
- new_kv_master: float32 [8192, 2048], P('dp', 'tensor')
- new_kv_first: float32 [8192, 2048], P('dp', 'tensor')
- new_kv_second: float32 [8192, 2048], P('dp', 'tensor')
- new_out_master: float32 [8192, 4096], P('dp', 'tensor')
- new_out_first: float32 [8192, 4096], P('dp', 'tensor')
- new_out_second: float32 [8192, 4096], P('dp', 'tensor')
- next_keyvalue: bfloat16 [4096, 2048], P('dp', 'tensor')
- next_output: bfloat16 [4096, 8192], P('dp', 'tensor')
All inputs are finite; a program needn't handle non-finite values.
Results may differ from a plain program's by a relative error of at most 0.025.
Values may be sent and summed in bfloat16 or wider, within the bound.
No kernel may reach another device: no remote copies, remote signals or barrier semaphores. Data moves between devices by JAX's collectives and lax.ppermute only.
A program may use at most 128 MiB of HBM per device.

v0:
```python
import math

import jax
import jax.numpy as jnp
from jax import lax
from jax.sharding import PartitionSpec as P

D = 8192
STEP = 10
KVW = 2048
QD = 4096


beta_one = 0.9
beta_two = 0.95
learn_rate = 0.01
weight_decay = 0.1
epsilon = 1e-08
clip_ratio = 0.25


def adam_update(master, first_moment, second_moment, gradient, factor):
    scaled = gradient * factor
    first_moment = beta_one * first_moment + (1.0 - beta_one) * scaled
    second_moment = beta_two * second_moment + (1.0 - beta_two) * scaled * scaled
    first_hat = first_moment / (1.0 - beta_one**STEP)
    second_hat = second_moment / (1.0 - beta_two**STEP)
    direction = first_hat / (jnp.sqrt(second_hat) + epsilon)
    master = master - learn_rate * (direction + weight_decay * master)
    return (master, first_moment, second_moment)


def contract_tokens(left, right):
    return lax.dot_general(
        left, right, (((0,), (0,)), ((), ())), preferred_element_type=jnp.float32
    )


def contract_columns(left, right):
    return lax.dot_general(
        left, right, (((1,), (1,)), ((), ())), preferred_element_type=jnp.float32
    )


def scatter_kv(term_fn, own_rows):
    return lax.psum_scatter(
        term_fn(jnp.int32(0), own_rows * lax.axis_size("dp")).astype(jnp.bfloat16),
        "dp",
        scatter_dimension=0,
        tiled=True,
    ).astype(jnp.float32)


def scatter_out(term_fn, own_rows):
    return lax.psum_scatter(
        term_fn(jnp.int32(0), own_rows * lax.axis_size("dp")).astype(jnp.bfloat16),
        "dp",
        scatter_dimension=0,
        tiled=True,
    ).astype(jnp.float32)


def whole_total(value):
    return lax.psum(value, ("dp", "tensor"))


def body(
    enc_states,
    kv_cotangent,
    out_cotangent,
    attn_context,
    next_states,
    next_context,
    kv_master,
    kv_first,
    kv_second,
    out_master,
    out_first,
    out_second,
):
    own_rows = kv_master.shape[0]
    kv_scale = D ** (-0.5)
    out_scale = QD ** (-0.5)
    max_norm = clip_ratio * math.sqrt(D * (KVW + QD))

    def kv_term(offset, extent):
        return contract_tokens(enc_states, kv_cotangent) * kv_scale

    def out_term(offset, extent):
        return contract_tokens(out_cotangent, attn_context) * out_scale

    kv_grad = scatter_kv(kv_term, own_rows)
    kv_squares = jnp.sum(kv_grad * kv_grad)
    out_grad = scatter_out(out_term, own_rows)
    squares_total = whole_total(kv_squares + jnp.sum(out_grad * out_grad))
    factor = jnp.minimum(1.0, max_norm / (jnp.sqrt(squares_total) + 1e-06))
    new_kv_master, new_kv_first, new_kv_second = adam_update(
        kv_master, kv_first, kv_second, kv_grad, factor
    )
    new_out_master, new_out_first, new_out_second = adam_update(
        out_master, out_first, out_second, out_grad, factor
    )
    kv_weight = new_kv_master.astype(jnp.bfloat16)
    out_weight = new_out_master.astype(jnp.bfloat16)
    keyvalue = jnp.dot(
        next_states,
        lax.all_gather(kv_weight, "dp", axis=0, tiled=True),
        preferred_element_type=jnp.float32,
    )
    next_keyvalue = keyvalue.astype(jnp.bfloat16)
    partial_out = contract_columns(
        next_context, lax.all_gather(out_weight, "dp", axis=0, tiled=True)
    )
    next_output = lax.psum_scatter(
        partial_out.astype(jnp.bfloat16), "tensor", scatter_dimension=1, tiled=True
    )
    return (
        new_kv_master,
        new_kv_first,
        new_kv_second,
        new_out_master,
        new_out_first,
        new_out_second,
        next_keyvalue,
        next_output,
    )


def solution(mesh):
    return jax.shard_map(
        body,
        mesh=mesh,
        in_specs=(
            P("dp", None),
            P("dp", "tensor"),
            P("dp", None),
            P("dp", "tensor"),
            P("dp", None),
            P("dp", "tensor"),
            P("dp", "tensor"),
            P("dp", "tensor"),
            P("dp", "tensor"),
            P("dp", "tensor"),
            P("dp", "tensor"),
            P("dp", "tensor"),
        ),
        out_specs=(
            P("dp", "tensor"),
            P("dp", "tensor"),
            P("dp", "tensor"),
            P("dp", "tensor"),
            P("dp", "tensor"),
            P("dp", "tensor"),
            P("dp", "tensor"),
            P("dp", "tensor"),
        ),
        check_vma=False,
    )
```

profile of v0, /device:TPU:15, one launch (start us, length us, event | category | flops | bytes accessed | tf_op | source)
XLA Modules:
  0.0 825.7 jit_solution(4256715491643386978)
XLA Ops:
  7.2 0.0 copy-start
  7.2 0.0 reduce-scatter.4.cloned.1.call-start
  7.2 5.0 fusion
  12.2 0.0 copy-start.5
  12.2 0.0 reduce-scatter.4.cloned.1.call-update
  12.2 0.0 reduce-scatter.6.cloned.1.call-start
  12.3 0.0 copy-done
  12.3 0.8 copy-done.5
  13.1 5.6 multiply_convert_fusion
  18.7 0.0 copy-start.1
  18.7 0.0 copy-start.2
  18.7 0.0 reduce-scatter.6.cloned.1.call-update
  18.7 0.0 copy-start.4
  18.7 0.0 all-gather.5.cloned.1.call-start
  18.8 129.6 %reduce-scatter.4.cloned.1.call-done = bf16[256,256]{1,0:T(8,128)(2,1)} async-done(((bf16[8192,256]{1,0:T(8,128)(2,1)}), bf16[256,256]{1,0:T(8,128)(2,1)}) %reduce-scatter.4.cloned.1.call-update) | async-done | bytes 131088 | tf_op jit(solution)/shard_map/reduce_scatter | solution.py:46
  148.4 0.0 copy-start.3
  148.4 1.6 fusion.9
  150.0 178.7 %reduce-scatter.6.cloned.1.call-done = bf16[256,512]{1,0:T(8,128)(2,1)} async-done(((bf16[8192,512]{1,0:T(8,128)(2,1)}), bf16[256,512]{1,0:T(8,128)(2,1)}) %reduce-scatter.6.cloned.1.call-update) | async-done | bytes 262160 | tf_op jit(solution)/shard_map/reduce_scatter | solution.py:55
  328.7 1.7 fusion.5
  331.7 106.2 %psum.7 = f32[]{:T(128)} all-reduce(f32[]{:T(128)S(6)} %add.44), channel_id=1, replica_groups=mesh['dp'=32,'tensor'=8] {'dp','tensor'}, use_global_device_ids=true, to_apply=%region_4.0 | all-reduce | flops 1 | bytes 8 | tf_op jit(solution)/shard_map/psum | solution.py:64
  438.7 0.0 copy-done.1
  438.7 0.0 copy-done.2
  438.7 2.6 fusion.11
  441.3 0.0 all-gather.5.cloned.1.call-update
  441.4 0.0 all-gather.3.cloned.1.call-start
  441.4 0.0 copy-done.4
  441.4 0.0 copy-done.3
  441.4 2.1 fusion.14
  443.5 0.0 all-gather.3.cloned.1.call-update
  443.5 0.0 reduce-scatter.8.cloned.1.call-start
  443.6 140.1 %all-gather.5.cloned.1.call-done = bf16[8192,512]{1,0:T(8,128)(2,1)} async-done(((bf16[256,512]{1,0:T(8,128)(2,1)}), bf16[8192,512]{1,0:T(8,128)(2,1)}) %all-gather.5.cloned.1.call-update) | async-done | bytes 8388624 | tf_op jit(solution)/shard_map/all_gather | solution.py:112
  583.7 7.1 fusion.1
  590.8 0.0 reduce-scatter.8.cloned.1.call-update
  590.8 153.7 %all-gather.3.cloned.1.call-done = bf16[8192,256]{1,0:T(8,128)(2,1)} async-done(((bf16[256,256]{1,0:T(8,128)(2,1)}), bf16[8192,256]{1,0:T(8,128)(2,1)}) %all-gather.3.cloned.1.call-update) | async-done | bytes 4194320 | tf_op jit(solution)/shard_map/all_gather | solution.py:107
  744.5 4.2 fusion.2
  748.6 0.7 copy.20
  749.4 68.0 %reduce-scatter.8.cloned.1.call-done = bf16[128,1024]{0,1:T(8,128)(2,1)} async-done(((bf16[128,8192]{0,1:T(8,128)(2,1)}), bf16[128,1024]{0,1:T(8,128)(2,1)}) %reduce-scatter.8.cloned.1.call-update) | async-done | bytes 262160 | tf_op jit(solution)/shard_map/reduce_scatter | solution.py:114
  817.4 1.8 copy.21
Async XLA Ops:
  7.2 5.1 copy-start
  7.2 141.2 %reduce-scatter.4.cloned.1.call-start = ((), (), s32[]{:S(2)}) async-start(), calls=%async_computation.3 | async-start | bytes 4325376 | tf_op jit(solution)/shard_map/reduce_scatter | solution.py:46
  12.2 0.9 copy-start.5
  12.2 316.5 %reduce-scatter.6.cloned.1.call-start = ((), (), s32[]{:S(2)}) async-start(), calls=%async_computation.4 | async-start | bytes 8650752 | tf_op jit(solution)/shard_map/reduce_scatter | solution.py:55
  18.7 420.0 %copy-start.1 = (f32[256,512]{1,0:T(8,128)S(1)}, f32[256,512]{1,0:T(8,128)}, u32[]{:S(2)}) copy-start(f32[256,512]{1,0:T(8,128)} %param.21) | copy-start | bytes 1572868
  18.7 420.0 %copy-start.2 = (f32[256,512]{1,0:T(8,128)S(1)}, f32[256,512]{1,0:T(8,128)}, u32[]{:S(2)}) copy-start(f32[256,512]{1,0:T(8,128)} %param.22) | copy-start | bytes 1572868
  18.7 422.7 %copy-start.4 = (f32[256,256]{1,0:T(8,128)S(1)}, f32[256,256]{1,0:T(8,128)}, u32[]{:S(2)}) copy-start(f32[256,256]{1,0:T(8,128)} %param.18) | copy-start | bytes 786436
  18.7 565.0 %all-gather.5.cloned.1.call-start = ((), (), s32[]{:S(2)}) async-start(), calls=%async_computation.6 | async-start | bytes 8650752 | tf_op jit(solution)/shard_map/all_gather | solution.py:112
  148.4 293.0 %copy-start.3 = (bf16[256,256]{1,0:T(8,128)(2,1)S(1)}, bf16[256,256]{1,0:T(8,128)(2,1)}, u32[]{:S(2)}) copy-start(bf16[256,256]{1,0:T(8,128)(2,1)} %reduce-scatter.4.cloned.1.call-done) | copy-start | bytes 393220
  441.4 303.1 %all-gather.3.cloned.1.call-start = ((), (), s32[]{:S(2)}) async-start(), calls=%async_computation.5 | async-start | bytes 4325376 | tf_op jit(solution)/shard_map/all_gather | solution.py:107
  443.5 373.9 %reduce-scatter.8.cloned.1.call-start = ((), (), s32[]{:S(2)}) async-start(), calls=%async_computation.7 | async-start | bytes 2359296 | tf_op jit(solution)/shard_map/reduce_scatter | solution.py:114
Sparse Core Ops, SparseCore 0:
  12.3 135.9 reduce-scatter.3
  150.9 177.7 reduce-scatter.5
  441.5 142.1 all-gather.4
  585.4 159.0 all-gather.2
  746.9 70.4 reduce-scatter.7
where the time goes:
time: 828 us; the launch traced here: 826 us
  waiting for transfers between devices  670 us (81%)
  blocking collectives  106 us (13%)
  matrix products  21.8 us (3%)
  between operations  15.9 us (2%)
    reduce_scatter x1, waiting for transfers between devices, scatter_out(): lax.psum_scatter(term_fn(jnp.int32(0), own_rows * lax.axis_size('dp')).as...  179 us
    all_gather x1, waiting for transfers between devices, body(): lax.all_gather(kv_weight, 'dp', axis=0, tiled=True)  154 us
    all_gather x1, waiting for transfers between devices, body(): lax.all_gather(out_weight, 'dp', axis=0, tiled=True)  140 us
    reduce_scatter x1, waiting for transfers between devices, scatter_kv(): lax.psum_scatter(term_fn(jnp.int32(0), own_rows * lax.axis_size('dp')).as...  130 us
    psum x1, blocking collectives, whole_total(): return lax.psum(value, ('dp', 'tensor'))  106 us
    reduce_scatter x1, waiting for transfers between devices, body(): lax.psum_scatter(partial_out.astype(jnp.bfloat16), 'tensor', scatter_dime...  68 us
  transfers between devices with their start and end apart: 5, of which 5 were waited for; matrix products, arithmetic and copies ran while one was open for 3% of the time, Pallas kernels for 0%

commit v1 on v0

v1 whole, which is shorter than its diff:
```python
import itertools
import math

import jax
import jax.numpy as jnp
from jax import lax
from jax.experimental import pallas as pl
from jax.experimental.pallas import tpu as pltpu
from jax.sharding import PartitionSpec as P

D = 8192
STEP = 10
KVW = 2048
QD = 4096

NX, NZ, NY = 4, 2, 4
NH, NC = 4, 2
TOK = 128
HALF = TOK // 2
ROWS = 256
WIDE = NX * ROWS

beta_one = 0.9
beta_two = 0.95
learn_rate = 0.01
weight_decay = 0.1
epsilon = 1e-08
clip_ratio = 0.25


def dp_of(x, z, y):
    return (x * NZ + z) * NY + y


ZY_GROUPS = [[dp_of(x, z, y) for z in range(NZ) for y in range(NY)] for x in range(NX)]


def device_pairs(target):
    pairs = []
    for x, z, y, h, c in itertools.product(
        range(NX), range(NZ), range(NY), range(NH), range(NC)
    ):
        tx, tz, ty, th, tc = target(x, z, y, h, c)
        source = (dp_of(x, z, y) * NH + h) * NC + c
        pairs.append((source, (dp_of(tx % NX, tz % NZ, ty % NY) * NH + th % NH) * NC + tc % NC))
    return pairs


def move(values, target):
    return lax.ppermute(values, ("dp", "tensor"), device_pairs(target))


def move_core(values):
    return move(values, lambda x, z, y, h, c: (x, z, y, h, c + 1))


def move_x(values, k):
    return move(values, lambda x, z, y, h, c: (x + k, z, y, h, c))


def move_y(values, k):
    return move(values, lambda x, z, y, h, c: (x, z, y + k, h, c))


def move_h(values, k):
    return move(values, lambda x, z, y, h, c: (x, z, y, h + k, c))


def move_z(values):
    return move(values, lambda x, z, y, h, c: (x, z + 1, y, h, c))


def swap_xh(values):
    return move(values, lambda x, z, y, h, c: (h, z, y, x, c))


def move_home(values, k):
    return move(values, lambda x, z, y, h, c: (x + k, c, y, h, z))


def adam_update(master, first_moment, second_moment, gradient, factor):
    scaled = gradient * factor
    first_moment = beta_one * first_moment + (1.0 - beta_one) * scaled
    second_moment = beta_two * second_moment + (1.0 - beta_two) * scaled * scaled
    first_hat = first_moment / (1.0 - beta_one**STEP)
    second_hat = second_moment / (1.0 - beta_two**STEP)
    direction = first_hat / (jnp.sqrt(second_hat) + epsilon)
    master = master - learn_rate * (direction + weight_decay * master)
    return (master, first_moment, second_moment)


def dot(left, right, left_dims, right_dims):
    return lax.dot_general(
        left,
        right,
        ((left_dims, right_dims), ((), ())),
        preferred_element_type=jnp.float32,
    )


VMEM = pl.BlockSpec(memory_space=pltpu.VMEM)
SMEM = pl.BlockSpec(memory_space=pltpu.SMEM)


def call(kernel, out_shape, operands, scalars=(), flops=0, scratch=()):
    moved = sum(o.size * o.dtype.itemsize for o in (*operands, *jax.tree.leaves(out_shape)))
    return pl.pallas_call(
        kernel,
        out_shape=out_shape,
        in_specs=[SMEM] * len(scalars) + [VMEM] * len(operands),
        out_specs=jax.tree.map(lambda _: VMEM, out_shape),
        scratch_shapes=list(scratch),
        compiler_params=pltpu.CompilerParams(vmem_limit_bytes=40 * 2**20),
        cost_estimate=pl.CostEstimate(flops=flops, bytes_accessed=moved, transcendentals=0),
    )(*scalars, *operands)


def shape(dims, dtype=jnp.bfloat16):
    return jax.ShapeDtypeStruct(dims, dtype)


def contract(left, right, left_dim, right_dim):
    return lax.dot_general(
        left, right, (((left_dim,), (right_dim,)), ((), ())), preferred_element_type=jnp.float32
    )


def halves(core):
    own = pl.ds(pl.multiple_of(core * HALF, HALF), HALF)
    other = pl.ds(pl.multiple_of((1 - core) * HALF, HALF), HALF)
    return own, other


def columns_of(x, k, p=None):
    first = lax.rem(x + k, NX) * (NZ * NY)
    if p is None:
        return pl.ds(pl.multiple_of(first * ROWS, ROWS), NZ * NY * ROWS)
    return pl.ds(pl.multiple_of((first + p) * ROWS, ROWS), ROWS)


def kv_payload(place, enc_states, kv_cotangent):
    width = NZ * NY * ROWS
    kvw = kv_cotangent.shape[1]

    def kernel(place_ref, states_ref, cot_ref, o0, o1, o2, o3, rest_ref):
        x, core = place_ref[0], place_ref[4]
        own, other = halves(core)
        for k, out_ref in enumerate((o0, o1, o2, o3)):
            out_ref[:, :width] = states_ref[own, columns_of(x, k)]
            out_ref[:, width : width + kvw] = cot_ref[own, :]
            out_ref[:, width + kvw :] = cot_ref[other, :]
        rest_ref[...] = states_ref[other, columns_of(x, 0)]

    out_shape = (shape((HALF, width + 2 * kvw)),) * NX + (shape((HALF, width)),)
    return call(kernel, out_shape, (enc_states, kv_cotangent), (place,))


def out_payload(place, out_cotangent, attn_context):
    qd = attn_context.shape[1]

    def kernel(place_ref, cot_ref, context_ref, out_ref):
        x, core = place_ref[0], place_ref[4]
        own, other = halves(core)
        for p in range(NZ * NY):
            for k in range(NX):
                rows = slice((k // 2) * HALF, (k // 2 + 1) * HALF)
                cols = slice((k % 2) * ROWS, (k % 2 + 1) * ROWS)
                out_ref[p, rows, cols] = cot_ref[own, columns_of(x, k, p)]
            out_ref[p, :HALF, 2 * ROWS :] = context_ref[own, :]
            out_ref[p, HALF:, 2 * ROWS :] = context_ref[other, :]

    out_shape = shape((NZ * NY, TOK, 2 * ROWS + qd))
    return call(kernel, out_shape, (out_cotangent, attn_context), (place,))


def kv_terms(place, own, other, next_states, kvw, scale):
    width = NZ * NY * ROWS

    def kernel(place_ref, *refs):
        own_refs, other_refs, states_ref, out_ref = (
            refs[:NX],
            refs[NX : 2 * NX],
            refs[2 * NX],
            refs[2 * NX + 1],
        )
        x, core = place_ref[0], place_ref[4]
        half, _ = halves(core)
        own_cot = jnp.concatenate([r[:, width : width + kvw] for r in own_refs], axis=0)
        other_cot = jnp.concatenate([r[:, width + kvw :] for r in own_refs], axis=0)
        for p in range(NZ * NY):
            cols = slice(p * ROWS, (p + 1) * ROWS)
            term = contract(own_cot, jnp.concatenate([r[:, cols] for r in own_refs]), 0, 0)
            term += contract(other_cot, jnp.concatenate([r[:, cols] for r in other_refs]), 0, 0)
            out_ref[p, :kvw] = (term * scale).astype(jnp.bfloat16)
            for k in range(NX):
                rows = slice(kvw + k * HALF, kvw + (k + 1) * HALF)
                out_ref[p, rows] = states_ref[half, columns_of(x, k, p)]

    out_shape = shape((NZ * NY, kvw + NX * HALF, ROWS))
    return call(kernel, out_shape, (*own, *other, next_states), (place,), flops=2**29)


def out_terms(own, other, qd, scale):
    tokens = NZ * NY * HALF

    def kernel(own_ref, other_ref, *out_refs):
        own_context = own_ref[:, :HALF, 2 * ROWS :].reshape(tokens, qd)
        other_context = own_ref[:, HALF:, 2 * ROWS :].reshape(tokens, qd)
        for k, out_ref in enumerate(out_refs):
            rows = slice((k // 2) * HALF, (k // 2 + 1) * HALF)
            cols = slice((k % 2) * ROWS, (k % 2 + 1) * ROWS)
            term = contract(own_context, own_ref[:, rows, cols].reshape(tokens, ROWS), 0, 0)
            term += contract(other_context, other_ref[:, rows, cols].reshape(tokens, ROWS), 0, 0)
            out_ref[...] = (term * scale).astype(jnp.bfloat16)

    return call(kernel, (shape((qd, ROWS)),) * NX, (own, other), flops=2**30)


def sum_terms(terms, columns):
    rows = terms[0].shape[-1]

    def kernel(*refs):
        *term_refs, grad_ref, squares_ref = refs
        total = None
        for ref in term_refs:
            parts = [ref[...]] if len(ref.shape) == 2 else [ref[i, :columns] for i in range(ref.shape[0])]
            for part in parts:
                part = part.astype(jnp.float32)
                total = part if total is None else total + part
        squares_ref[0, 0] = jnp.sum(total * total)
        grad_ref[...] = total.T

    return pl.pallas_call(
        kernel,
        out_shape=(shape((rows, columns), jnp.float32), shape((1, 1), jnp.float32)),
        in_specs=[VMEM] * len(terms),
        out_specs=(VMEM, SMEM),
        compiler_params=pltpu.CompilerParams(vmem_limit_bytes=40 * 2**20),
        cost_estimate=pl.CostEstimate(flops=2**20, bytes_accessed=2**20, transcendentals=0),
    )(*terms)


def next_partial(place, which, context, weights, arrived=None):
    qd = context[0].shape[-1]
    n_in = NH + NY

    def kernel(place_ref, which_ref, *refs):
        x, y, h = place_ref[0], place_ref[2], place_ref[3]
        *refs, tokens_ref = refs
        outs = refs[n_in + (arrived is not None) :]
        for j in range(NH):
            tokens_ref[lax.rem(h - j - x + 2 * NX, NX)] = refs[j][which_ref[0]]
        tokens = tokens_ref[...].reshape(NX * TOK, qd)
        for j in range(NY):
            cols = pl.ds(pl.multiple_of(lax.rem(y - j + NY, NY) * ROWS, ROWS), ROWS)
            part = contract(tokens, refs[NH + j][...], 1, 1)
            if arrived is None:
                outs[0][:, cols] = part.astype(jnp.bfloat16)
            else:
                part += refs[n_in][:, cols].astype(jnp.float32)
                for k in range(NX):
                    outs[k][:, cols] = part[k * TOK : (k + 1) * TOK].astype(jnp.bfloat16)

    if arrived is None:
        out_shape = (shape((NX * TOK, NY * ROWS)),)
        operands = (*context, *weights)
    else:
        out_shape = (shape((TOK, NY * ROWS)),) * NX
        operands = (*context, *weights, arrived)
    scratch = [pltpu.VMEM((NX, TOK, qd), jnp.bfloat16)]
    return call(kernel, out_shape, operands, (place, which), 2**29, scratch)


def keyvalue_partial(own, other, weights):
    kvw = weights[0].shape[1]

    def kernel(own_ref, other_ref, w0, w1, w2, w3, out_ref):
        for half, ref in enumerate((own_ref, other_ref)):
            total = None
            for j, weight in enumerate((w0, w1, w2, w3)):
                first = ref.shape[1] - (NX - -j % NX) * HALF
                block = ref[:, first : first + HALF].reshape(NZ * NY * HALF, ROWS)
                part = contract(block, weight[...], 1, 0)
                total = part if total is None else total + part
            out_ref[:, half * HALF : (half + 1) * HALF] = total.astype(jnp.bfloat16).reshape(
                NZ * NY, HALF, kvw
            )

    return call(kernel, shape((NZ * NY, TOK, kvw)), (own, other, *weights), flops=2**29)


def to_set(values):
    return lax.all_to_all(values, "dp", 0, 0, axis_index_groups=ZY_GROUPS)


def body(
    enc_states,
    kv_cotangent,
    out_cotangent,
    attn_context,
    next_states,
    next_context,
    kv_master,
    kv_first,
    kv_second,
    out_master,
    out_first,
    out_second,
):
    bf16, f32 = jnp.bfloat16, jnp.float32
    after = lax.optimization_barrier
    dp, tensor = lax.axis_index("dp"), lax.axis_index("tensor")
    x, z, y = dp // (NZ * NY), (dp // NY) % NZ, dp % NY
    h, core = tensor // NC, tensor % NC
    kv_scale = D ** (-0.5)
    out_scale = QD ** (-0.5)
    max_norm = clip_ratio * math.sqrt(D * (KVW + QD))
    kvw, qd = kv_cotangent.shape[1], attn_context.shape[1]
    place = jnp.stack([x, z, y, h, core]).astype(jnp.int32)
    kept_half = (core ^ z).astype(jnp.int32).reshape(1)

    out_sent = out_payload(place, out_cotangent, attn_context)
    out_landed = to_set(out_sent)
    place_kv, out_sent = after((place, out_sent))
    *kv_sent, kv_rest = kv_payload(place_kv, enc_states, kv_cotangent)
    kv_own = [kv_sent[0]] + [move_x(kv_sent[k], k) for k in range(1, NX)]
    context = swap_xh(next_context)
    kv_other = [kv_rest] + [move_core(part) for part in kv_own[1:]]

    kv_part = kv_terms(place, kv_own, kv_other, next_states, kvw, kv_scale)
    kv_part, out_landed, context = after((kv_part, out_landed, context))
    kv_landed = to_set(kv_part)
    out_other = move_core(out_landed[:, :, : 2 * ROWS])
    out_parts = out_terms(out_landed, out_other, qd, out_scale)
    context_z = move_z(context)
    out_parts = [out_parts[0]] + [move_x(out_parts[k], k) for k in range(1, NX)]
    out_grad, out_squares = sum_terms(out_parts, qd)
    kv_landed, out_squares, context_z = after((kv_landed, out_squares, context_z))
    context = jnp.stack([context, context_z])
    context = [context] + [move_h(context, j) for j in range(1, NH)]
    kv_grad, kv_squares = sum_terms([kv_landed], kvw)
    states_other = move_core(kv_landed[:, kvw:])

    n_all = NX * NZ * NY * NH * NC
    squares_all = lax.all_to_all(
        jnp.broadcast_to((kv_squares + out_squares).reshape(1, 1, 1), (n_all, 1, 128)),
        ("dp", "tensor"),
        0,
        0,
    )
    squares_all, context, states_other = after((squares_all, context, states_other))
    squares_total = jnp.sum(squares_all[:, 0, 0])
    factor = jnp.minimum(1.0, max_norm / (jnp.sqrt(squares_total) + 1e-06))
    new_out_master, new_out_first, new_out_second = adam_update(
        out_master, out_first, out_second, out_grad, factor
    )
    new_kv_master, new_kv_first, new_kv_second = adam_update(
        kv_master, kv_first, kv_second, kv_grad, factor
    )

    out_weight = swap_xh(new_out_master.astype(bf16))
    out_weight, kv_weight = after((out_weight, new_kv_master.astype(bf16)))
    out_weights = [out_weight] + [move_y(out_weight, j) for j in range(1, NY)]
    kv_weights = [kv_weight] + [move_x(kv_weight, j) for j in range(1, NX)]
    out_weights, kv_weights = after((out_weights, kv_weights))
    (sent,) = next_partial(place, 1 - kept_half, context, out_weights)
    arrived = move_core(sent)
    keyvalue = keyvalue_partial(kv_landed, states_other, kv_weights)
    arrived, keyvalue = after((arrived, keyvalue))
    kept = next_partial(place, kept_half, context, out_weights, arrived)
    homes = [move_home(block, k) for k, block in enumerate(kept)]
    homes[0], keyvalue = after((homes[0], keyvalue))
    next_output = sum(part.astype(f32) for part in homes).astype(bf16)

    keyvalue = to_set(keyvalue)
    keyvalue = jnp.sum(keyvalue.astype(f32), axis=0).astype(bf16)
    next_keyvalue = jnp.where(core == 0, keyvalue, jnp.roll(keyvalue, HALF, axis=0))
    return (
        new_kv_master,
        new_kv_first,
        new_kv_second,
        new_out_master,
        new_out_first,
        new_out_second,
        next_keyvalue,
        next_output,
    )


def solution(mesh):
    return jax.shard_map(
        body,
        mesh=mesh,
        in_specs=(
            P("dp", None),
            P("dp", "tensor"),
            P("dp", None),
            P("dp", "tensor"),
            P("dp", None),
            P("dp", "tensor"),
            P("dp", "tensor"),
            P("dp", "tensor"),
            P("dp", "tensor"),
            P("dp", "tensor"),
            P("dp", "tensor"),
            P("dp", "tensor"),
        ),
        out_specs=(
            P("dp", "tensor"),
            P("dp", "tensor"),
            P("dp", "tensor"),
            P("dp", "tensor"),
            P("dp", "tensor"),
            P("dp", "tensor"),
            P("dp", "tensor"),
            P("dp", "tensor"),
        ),
        check_vma=False,
    )
```

time: 828 us -> 204 us (0.25)
  waiting for transfers between devices: 670 us -> 76.3 us
  blocking collectives: 106 us -> 26.3 us
  starting transfers between devices: 0.21 us -> 65.2 us
  matrix products: 21.8 us -> 0 us
  Pallas kernels: 0 us -> 13.1 us
  between operations: 15.9 us -> 2.99 us
    reduce_scatter x3 -> x0, waiting for transfers between devices: 376 us -> none  [the longest x1 179 us: scatter_out(): lax.psum_scatter(term_fn(jnp.int32(0), own_rows * lax.axis_size('dp')).as...]
    all_gather x2 -> x0, waiting for transfers between devices: 294 us -> none  [the longest x1 154 us: body(): lax.all_gather(kv_weight, 'dp', axis=0, tiled=True)]
    psum x1 -> x0, blocking collectives: 106 us -> none  [whole_total(): return lax.psum(value, ('dp', 'tensor'))]
    ppermute x0 -> x28, waiting for transfers between devices: none -> 76.3 us  [move(): return lax.ppermute(values, ('dp', 'tensor'), device_pairs(target))]
    ppermute x0 -> x28, starting transfers between devices: none -> 47.5 us  [move(): return lax.ppermute(values, ('dp', 'tensor'), device_pairs(target))]
    all_to_all x0 -> x1, blocking collectives: none -> 26.3 us  [body(): lax.all_to_all(jnp.broadcast_to((kv_squares + out_squares).reshape(1, 1,...]
    dot_general x4 -> x0, matrix products: 21.8 us -> none  [the longest x2 10.6 us: contract_tokens(): lax.dot_general(left, right, (((0,), (0,)), ((), ())), preferred_element_...]
    all_to_all x0 -> x3, starting transfers between devices: none -> 17.7 us  [to_set(): return lax.all_to_all(values, 'dp', 0, 0, axis_index_groups=ZY_GROUPS)]
  transfers between devices with their start and end apart: 5 -> 31, of which waited for: 5 -> 15; matrix products, arithmetic and copies ran while one was open for 3% -> 2% of each run, Pallas kernels for 0% -> 4%
where the time goes in v1:
time: 204 us; the launch traced here: 202 us
  waiting for transfers between devices  76.3 us (37%)
  starting transfers between devices  65.2 us (32%)
  blocking collectives  26.3 us (13%)
  Pallas kernels  13.1 us (6%)
  local copies, waits for them, and re-layouts  10.9 us (5%)
  other arithmetic  7.6 us (4%)
  between operations  2.99 us (1%)
    ppermute x28, waiting for transfers between devices, move(): return lax.ppermute(values, ('dp', 'tensor'), device_pairs(target))  76.3 us
    ppermute x28, starting transfers between devices, move(): return lax.ppermute(values, ('dp', 'tensor'), device_pairs(target))  47.5 us
    all_to_all x1, blocking collectives, body(): lax.all_to_all(jnp.broadcast_to((kv_squares + out_squares).reshape(1, 1,...  26.3 us
    all_to_all x3, starting transfers between devices, to_set(): return lax.all_to_all(values, 'dp', 0, 0, axis_index_groups=ZY_GROUPS)  17.7 us
    pallas_call x7, Pallas kernels, call(): pl.pallas_call(kernel, out_shape=out_shape, in_specs=[SMEM] * len(scalars...  11.5 us
    unnamed x32, local copies, waits for them, and re-layouts  9.22 us
  transfers between devices with their start and end apart: 31, of which 15 were waited for; matrix products, arithmetic and copies ran while one was open for 2% of the time, Pallas kernels for 4%

profile of v1, /device:TPU:15, one launch (start us, length us, event | category | flops | bytes accessed | tf_op | source)
XLA Modules:
  0.0 202.4 jit_solution(2098264364381400476)
XLA Ops:
  0.8 1.6 copy-done.4
  3.3 2.1 %shard_map.179 = bf16[8,128,1024]{2,1,0:T(8,128)(2,1)} custom-call(s32[5]{0:T(128)S(1)} %stack.32.place_ref, bf16[128,8192]{1,0:T(8,128)(2,1)S(1)} %copy-done.4, bf16[128,512]{1,0:T(8,128)(2,1)S(1)} %copy-done.11), custom_call_target="tpu_custom_call" | custom-call | bytes 4325376 | tf_op jit(solution)/shard_map/pallas_call | solution.py:107
  5.4 5.8 %all-to-all-start = ((bf16[8,128,1024]{2,1,0:T(8,128)(2,1)}), bf16[8,128,1024]{2,1,0:T(8,128)(2,1)S(1)}, u32[]{:S(2)}, u32[]{:S(2)}) async-start(bf16[8,128,1024]{2,1,0:T(8,128)(2,1)} %shard_map.179), calls=%async_computation | async-start | bytes 4194304 | tf_op jit(solution)/shard_map/all_to_all | solution.py:293
  11.2 1.6 copy-done.3
  13.7 2.1 %collective-permute-start.1 = (bf16[64,2560]{1,0:T(8,128)(2,1)S(1)}, bf16[64,2560]{1,0:T(8,128)(2,1)S(1)}, u32[]{:S(2)}, u32[]{:S(2)}) collective-permute-start(bf16[64,2560]{1,0:T(8,128)(2,1)S(1)} %get-tuple-element.55), channel_id=1, source_target_pairs={{0,128},{1,129},{2,130},{3,131},{4,132},{5,133},{6,134},{7,135},{8... | collective-permute-start | bytes 983048 | tf_op jit(solution)/shard_map/ppermute | solution.py:50
  15.9 5.6 %collective-permute-done.refs_1_ = bf16[64,2560]{1,0:T(8,128)(2,1)S(1)} collective-permute-done((bf16[64,2560]{1,0:T(8,128)(2,1)S(1)}, bf16[64,2560]{1,0:T(8,128)(2,1)S(1)}, u32[]{:S(2)}, u32[]{:S(2)}) %collective-permute-start) | collective-permute-done | bytes 327712 | tf_op jit(solution)/shard_map/ppermute | solution.py:50
  21.5 3.9 %collective-permute-start.3 = (bf16[64,2560]{1,0:T(8,128)(2,1)S(1)}, bf16[64,2560]{1,0:T(8,128)(2,1)S(1)}, u32[]{:S(2)}, u32[]{:S(2)}) collective-permute-start(bf16[64,2560]{1,0:T(8,128)(2,1)S(1)} %collective-permute-done.refs_1_), channel_id=1, source_target_pairs={{0,1},{1,0},{2,3},{3,2},{4,5},{5,4},{6,7},{7,6},{8,9},{9,8},{10,11... | collective-permute-start | bytes 983048 | tf_op jit(solution)/shard_map/ppermute | solution.py:50
  25.4 2.0 collective-permute-start.4
  27.4 4.4 %collective-permute-done.2.refs_3_ = bf16[64,2560]{1,0:T(8,128)(2,1)S(1)} collective-permute-done((bf16[64,2560]{1,0:T(8,128)(2,1)S(1)}, bf16[64,2560]{1,0:T(8,128)(2,1)S(1)}, u32[]{:S(2)}, u32[]{:S(2)}) %collective-permute-start.2) | collective-permute-done | bytes 327712 | tf_op jit(solution)/shard_map/ppermute | solution.py:50
  32.4 7.4 %collective-permute-start.6 = (bf16[128,512]{1,0:T(8,128)(2,1)S(1)}, bf16[128,512]{1,0:T(8,128)(2,1)S(1)}, u32[]{:S(2)}, u32[]{:S(2)}) collective-permute-start(bf16[128,512]{1,0:T(8,128)(2,1)S(1)} %copy-done.15), channel_id=1, source_target_pairs={{0,0},{1,1},{2,64},{3,65},{4,128},{5,129},{6,192},{7,193},{8,8},{9... | collective-permute-start | bytes 393224 | tf_op jit(solution)/shard_map/ppermute | solution.py:50
  39.9 1.3 shard_map.181
  41.2 1.3 copy-done
  42.5 5.1 %collective-permute-done.6 = bf16[128,512]{1,0:T(8,128)(2,1)S(1)} collective-permute-done((bf16[128,512]{1,0:T(8,128)(2,1)S(1)}, bf16[128,512]{1,0:T(8,128)(2,1)S(1)}, u32[]{:S(2)}, u32[]{:S(2)}) %collective-permute-start.6) | collective-permute-done | bytes 131104 | tf_op jit(solution)/shard_map/ppermute | solution.py:50
  47.7 1.3 copy-done.1
  49.0 7.0 %all-to-all-start.1 = ((bf16[8,512,256]{2,1,0:T(8,128)(2,1)}), bf16[8,512,256]{2,1,0:T(8,128)(2,1)S(1)}, u32[]{:S(2)}, u32[]{:S(2)}) async-start(bf16[8,512,256]{2,1,0:T(8,128)(2,1)} %copy-done), calls=%async_computation.1 | async-start | bytes 4194304 | tf_op jit(solution)/shard_map/all_to_all | solution.py:293
  56.0 1.4 slice.17
  57.5 1.2 collective-permute-start.7
  58.7 2.3 %collective-permute-done.7.other_ref = bf16[8,128,512]{2,1,0:T(8,128)(2,1)S(1)} collective-permute-done((bf16[8,128,512]{2,1,0:T(8,128)(2,1)S(1)}, bf16[8,128,512]{2,1,0:T(8,128)(2,1)S(1)}, u32[]{:S(2)}, u32[]{:S(2)}) %collective-permute-start.7) | collective-permute-done | bytes 1048608 | tf_op jit(solution)/shard_map/ppermute | solution.py:50
  61.0 1.3 shard_map.182
  62.4 2.7 %collective-permute-start.8 = (bf16[512,256]{1,0:T(8,128)(2,1)S(1)}, bf16[512,256]{1,0:T(8,128)(2,1)S(1)}, u32[]{:S(2)}, u32[]{:S(2)}) collective-permute-start(bf16[512,256]{1,0:T(8,128)(2,1)S(1)} %get-tuple-element.61), channel_id=1, source_target_pairs={{0,64},{1,65},{2,66},{3,67},{4,68},{5,69},{6,70},{7,71},{8,72},{9,... | collective-permute-start | bytes 786440 | tf_op jit(solution)/shard_map/ppermute | solution.py:50
  65.0 1.2 collective-permute-start.11
  66.2 10.5 %collective-permute-done.10.refs_3_ = bf16[512,256]{1,0:T(8,128)(2,1)S(1)} collective-permute-done((bf16[512,256]{1,0:T(8,128)(2,1)S(1)}, bf16[512,256]{1,0:T(8,128)(2,1)S(1)}, u32[]{:S(2)}, u32[]{:S(2)}) %collective-permute-start.10) | collective-permute-done | bytes 262176 | tf_op jit(solution)/shard_map/ppermute | solution.py:50
  78.3 4.5 %collective-permute-done.11 = bf16[128,512]{1,0:T(8,128)(2,1)S(1)} collective-permute-done((bf16[128,512]{1,0:T(8,128)(2,1)S(1)}, bf16[128,512]{1,0:T(8,128)(2,1)S(1)}, u32[]{:S(2)}, u32[]{:S(2)}) %collective-permute-start.11) | collective-permute-done | bytes 131104 | tf_op jit(solution)/shard_map/ppermute | solution.py:50
  82.9 1.8 collective-permute-start.15
  84.8 2.4 %collective-permute-start.13 = (bf16[2,128,512]{2,1,0:T(8,128)(2,1)S(1)}, bf16[2,128,512]{2,1,0:T(8,128)(2,1)S(1)}, u32[]{:S(2)}, u32[]{:S(2)}) collective-permute-start(bf16[2,128,512]{2,1,0:T(8,128)(2,1)S(1)} %pad_maximum_fusion.refs_0_), channel_id=1, source_target_pairs={{0,4},{1,5},{2,6},{3,7},{4,0},{5,1},{6,2},{7,3},{8,12},{9,13},{10,... | collective-permute-start | bytes 786440 | tf_op jit(solution)/shard_map/ppermute | solution.py:50
  87.2 3.5 %collective-permute-start.14 = (bf16[2,128,512]{2,1,0:T(8,128)(2,1)S(1)}, bf16[2,128,512]{2,1,0:T(8,128)(2,1)S(1)}, u32[]{:S(2)}, u32[]{:S(2)}) collective-permute-start(bf16[2,128,512]{2,1,0:T(8,128)(2,1)S(1)} %pad_maximum_fusion.refs_0_), channel_id=1, source_target_pairs={{0,6},{1,7},{2,0},{3,1},{4,2},{5,3},{6,4},{7,5},{8,14},{9,15},{10,... | collective-permute-start | bytes 786440 | tf_op jit(solution)/shard_map/ppermute | solution.py:50
  92.9 26.3 %all_to_all.20 = f32[256,1,128]{2,1,0:T(1,128)S(1)} all-to-all(f32[256,1,128]{2,1,0:T(1,128)S(1)} %broadcast_in_dim.8), channel_id=1, replica_groups=mesh['dp'=32,'tensor'=8] {'dp','tensor'}, dimensions={0} | all-to-all | bytes 262144 | tf_op jit(solution)/shard_map/all_to_all | solution.py:345
  119.2 1.0 copy-done.6
  121.8 3.0 %fusion.4 = (bf16[256,512]{1,0:T(8,128)(2,1)S(1)}, f32[256,512]{1,0:T(8,128)}, f32[256,512]{1,0:T(8,128)}, f32[256,512]{1,0:T(8,128)}) fusion(f32[256,512]{1,0:T(8,128)} %param.21, f32[256,512]{1,0:T(8,128)} %copy-done.8, f32[]{:T(128)S(6)} %min_shard_map.3, f32[256,512]{1,0:T(8,128)} %param.22, f32[256,512]{1,0:T(8,128)} %param.23), kind=kLoop, calls=%fused_computation.13 | loop fusion | flops 2228224 | bytes 3932164 | tf_op jit(solution)/shard_map/convert_element_type | solution.py:361
  124.8 6.0 %collective-permute-start.16 = (bf16[256,512]{1,0:T(8,128)(2,1)S(1)}, bf16[256,512]{1,0:T(8,128)(2,1)S(1)}, u32[]{:S(2)}, u32[]{:S(2)}) collective-permute-start(bf16[256,512]{1,0:T(8,128)(2,1)S(1)} %get-tuple-element.100), channel_id=1, source_target_pairs={{0,0},{1,1},{2,64},{3,65},{4,128},{5,129},{6,192},{7,193},{8,8},{9... | collective-permute-start | bytes 786440 | tf_op jit(solution)/shard_map/ppermute | solution.py:50
  130.9 2.1 %fusion.2 = (bf16[256,256]{1,0:T(8,128)(2,1)S(1)}, f32[256,256]{1,0:T(8,128)}, f32[256,256]{1,0:T(8,128)}, f32[256,256]{1,0:T(8,128)}) fusion(f32[256,256]{1,0:T(8,128)} %param.18, f32[256,256]{1,0:T(8,128)S(1)} %copy-done.10, f32[]{:T(128)S(6)} %min_shard_map.3, f32[256,256]{1,0:T(8,128)} %param.19, f32[256,256]{1,0:T(8,128)} %param.20), kind=kLoop, calls=%fused_computation.12 | loop fusion | flops 1114112 | bytes 1966084 | tf_op jit(solution)/shard_map/convert_element_type | solution.py:362
  133.0 14.9 %collective-permute-done.16.refs_4_ = bf16[256,512]{1,0:T(8,128)(2,1)S(1)} collective-permute-done((bf16[256,512]{1,0:T(8,128)(2,1)S(1)}, bf16[256,512]{1,0:T(8,128)(2,1)S(1)}, u32[]{:S(2)}, u32[]{:S(2)}) %collective-permute-start.16) | collective-permute-done | bytes 262176 | tf_op jit(solution)/shard_map/ppermute | solution.py:50
  148.2 2.8 %collective-permute-start.18 = (bf16[256,512]{1,0:T(8,128)(2,1)S(1)}, bf16[256,512]{1,0:T(8,128)(2,1)}, u32[]{:S(2)}, u32[]{:S(2)}) collective-permute-start(bf16[256,512]{1,0:T(8,128)(2,1)S(1)} %collective-permute-done.16.refs_4_), channel_id=1, source_target_pairs={{0,16},{1,17},{2,18},{3,19},{4,20},{5,21},{6,22},{7,23},{8,24},{9,... | collective-permute-start | bytes 786440 | tf_op jit(solution)/shard_map/ppermute | solution.py:50
  151.3 1.0 collective-permute-done.20.w1
  153.3 3.3 %collective-permute-done.21.w2 = bf16[256,256]{1,0:T(8,128)(2,1)} collective-permute-done((bf16[256,256]{1,0:T(8,128)(2,1)S(1)}, bf16[256,256]{1,0:T(8,128)(2,1)}, u32[]{:S(2)}, u32[]{:S(2)}) %collective-permute-start.21) | collective-permute-done | bytes 131104 | tf_op jit(solution)/shard_map/ppermute | solution.py:50
  156.6 3.9 %collective-permute-done.22.w3 = bf16[256,256]{1,0:T(8,128)(2,1)} collective-permute-done((bf16[256,256]{1,0:T(8,128)(2,1)S(1)}, bf16[256,256]{1,0:T(8,128)(2,1)}, u32[]{:S(2)}, u32[]{:S(2)}) %collective-permute-start.22) | collective-permute-done | bytes 131104 | tf_op jit(solution)/shard_map/ppermute | solution.py:50
  160.5 3.1 %collective-permute-done.19.refs_7_ = bf16[256,512]{1,0:T(8,128)(2,1)} collective-permute-done((bf16[256,512]{1,0:T(8,128)(2,1)S(1)}, bf16[256,512]{1,0:T(8,128)(2,1)}, u32[]{:S(2)}, u32[]{:S(2)}) %collective-permute-start.19) | collective-permute-done | bytes 262176 | tf_op jit(solution)/shard_map/ppermute | solution.py:50
  163.6 1.9 shard_map.185
  166.1 2.5 %shard_map.186 = bf16[8,128,256]{2,1,0:T(8,128)(2,1)} custom-call(bf16[8,512,256]{2,1,0:T(8,128)(2,1)S(1)} %all-to-all-done.1.refs_0_.own_ref, bf16[8,256,256]{2,1,0:T(8,128)(2,1)S(1)} %copy-done.7, bf16[256,256]{1,0:T(8,128)(2,1)S(1)} %get-tuple-element.84.w0, bf16[256,256]{1,0:T(8,128)(2,1)S(1)} %copy-done.13, ...), custom_call_target="tpu_custom_call" | custom-call | flops 536870912 | bytes 4194304 | tf_op jit(solution)/shard_map/pallas_call | solution.py:107
  168.5 1.9 shard_map.187
  170.4 3.5 %collective-permute-start.24 = (bf16[128,1024]{1,0:T(8,128)(2,1)S(1)}, bf16[128,1024]{1,0:T(8,128)(2,1)S(1)}, u32[]{:S(2)}, u32[]{:S(2)}) collective-permute-start(bf16[128,1024]{1,0:T(8,128)(2,1)S(1)} %get-tuple-element.89), channel_id=1, source_target_pairs={{0,0},{1,32},{2,2},{3,34},{4,4},{5,36},{6,6},{7,38},{8,8},{9,40},{... | collective-permute-start | bytes 786440 | tf_op jit(solution)/shard_map/ppermute | solution.py:50
  173.9 4.1 %collective-permute-done.24 = bf16[128,1024]{1,0:T(8,128)(2,1)S(1)} collective-permute-done((bf16[128,1024]{1,0:T(8,128)(2,1)S(1)}, bf16[128,1024]{1,0:T(8,128)(2,1)S(1)}, u32[]{:S(2)}, u32[]{:S(2)}) %collective-permute-start.24) | collective-permute-done | bytes 262176 | tf_op jit(solution)/shard_map/ppermute | solution.py:50
  178.1 4.9 %all-to-all-start.3 = ((bf16[8,128,256]{2,1,0:T(8,128)(2,1)}), bf16[8,128,256]{2,1,0:T(8,128)(2,1)S(1)}, u32[]{:S(2)}, u32[]{:S(2)}) async-start(bf16[8,128,256]{2,1,0:T(8,128)(2,1)} %shard_map.186), calls=%async_computation.3 | async-start | bytes 1048576 | tf_op jit(solution)/shard_map/all_to_all | solution.py:293
  182.9 2.1 %collective-permute-start.25 = (bf16[128,1024]{1,0:T(8,128)(2,1)S(1)}, bf16[128,1024]{1,0:T(8,128)(2,1)S(1)}, u32[]{:S(2)}, u32[]{:S(2)}) collective-permute-start(bf16[128,1024]{1,0:T(8,128)(2,1)S(1)} %get-tuple-element.93), channel_id=1, source_target_pairs={{0,64},{1,96},{2,66},{3,98},{4,68},{5,100},{6,70},{7,102},{8,72},{... | collective-permute-start | bytes 786440 | tf_op jit(solution)/shard_map/ppermute | solution.py:50
  185.1 2.3 %collective-permute-start.26 = (bf16[128,1024]{1,0:T(8,128)(2,1)S(1)}, bf16[128,1024]{1,0:T(8,128)(2,1)S(1)}, u32[]{:S(2)}, u32[]{:S(2)}) collective-permute-start(bf16[128,1024]{1,0:T(8,128)(2,1)S(1)} %get-tuple-element.94), channel_id=1, source_target_pairs={{0,128},{1,160},{2,130},{3,162},{4,132},{5,164},{6,134},{7,166},{8... | collective-permute-start | bytes 786440 | tf_op jit(solution)/shard_map/ppermute | solution.py:50
  187.4 7.9 %collective-permute-done.25 = bf16[128,1024]{1,0:T(8,128)(2,1)S(1)} collective-permute-done((bf16[128,1024]{1,0:T(8,128)(2,1)S(1)}, bf16[128,1024]{1,0:T(8,128)(2,1)S(1)}, u32[]{:S(2)}, u32[]{:S(2)}) %collective-permute-start.25) | collective-permute-done | bytes 262176 | tf_op jit(solution)/shard_map/ppermute | solution.py:50
  195.3 3.6 %collective-permute-done.26 = bf16[128,1024]{1,0:T(8,128)(2,1)S(1)} collective-permute-done((bf16[128,1024]{1,0:T(8,128)(2,1)S(1)}, bf16[128,1024]{1,0:T(8,128)(2,1)S(1)}, u32[]{:S(2)}, u32[]{:S(2)}) %collective-permute-start.26) | collective-permute-done | bytes 262176 | tf_op jit(solution)/shard_map/ppermute | solution.py:50
  198.8 1.9 collective-permute-done.27
  (68 shorter events, 9.9 us)
Async XLA Ops:
  0.8 1.6 copy-start.4
  2.4 0.9 copy-start.11
  5.3 5.8 %copy-start.14 = (bf16[128,256]{1,0:T(8,128)(2,1)S(1)}, bf16[128,256]{1,0:T(8,128)(2,1)}, u32[]{:S(2)}) copy-start(bf16[128,256]{1,0:T(8,128)(2,1)} %cot_ref.3) | copy-start | bytes 196612
  5.3 27.0 %copy-start.15 = (bf16[128,512]{1,0:T(8,128)(2,1)S(1)}, bf16[128,512]{1,0:T(8,128)(2,1)}, u32[]{:S(2)}) copy-start(bf16[128,512]{1,0:T(8,128)(2,1)} %param.17) | copy-start | bytes 393220
  5.4 42.3 %all-to-all-start = ((bf16[8,128,1024]{2,1,0:T(8,128)(2,1)}), bf16[8,128,1024]{2,1,0:T(8,128)(2,1)S(1)}, u32[]{:S(2)}, u32[]{:S(2)}) async-start(bf16[8,128,1024]{2,1,0:T(8,128)(2,1)} %shard_map.179), calls=%async_computation | async-start | bytes 4194304 | tf_op jit(solution)/shard_map/all_to_all | solution.py:293
  11.2 1.6 copy-start.3
  12.8 27.1 %copy-start.5 = (bf16[128,8192]{1,0:T(8,128)(2,1)S(1)}, bf16[128,8192]{1,0:T(8,128)(2,1)}, u32[]{:S(2)}) copy-start(bf16[128,8192]{1,0:T(8,128)(2,1)} %refs_8_.1) | copy-start | bytes 6291460
  13.4 8.0 %collective-permute-start = (bf16[64,2560]{1,0:T(8,128)(2,1)S(1)}, bf16[64,2560]{1,0:T(8,128)(2,1)S(1)}, u32[]{:S(2)}, u32[]{:S(2)}) collective-permute-start(bf16[64,2560]{1,0:T(8,128)(2,1)S(1)} %get-tuple-element.54), channel_id=1, source_target_pairs={{0,64},{1,65},{2,66},{3,67},{4,68},{5,69},{6,70},{7,71},{8,72},{9,... | collective-permute-start | bytes 983048 | tf_op jit(solution)/shard_map/ppermute | solution.py:50
  13.7 11.7 %collective-permute-start.1 = (bf16[64,2560]{1,0:T(8,128)(2,1)S(1)}, bf16[64,2560]{1,0:T(8,128)(2,1)S(1)}, u32[]{:S(2)}, u32[]{:S(2)}) collective-permute-start(bf16[64,2560]{1,0:T(8,128)(2,1)S(1)} %get-tuple-element.55), channel_id=1, source_target_pairs={{0,128},{1,129},{2,130},{3,131},{4,132},{5,133},{6,134},{7,135},{8... | collective-permute-start | bytes 983048 | tf_op jit(solution)/shard_map/ppermute | solution.py:50
  15.9 16.0 %collective-permute-start.2 = (bf16[64,2560]{1,0:T(8,128)(2,1)S(1)}, bf16[64,2560]{1,0:T(8,128)(2,1)S(1)}, u32[]{:S(2)}, u32[]{:S(2)}) collective-permute-start(bf16[64,2560]{1,0:T(8,128)(2,1)S(1)} %get-tuple-element.56), channel_id=1, source_target_pairs={{0,192},{1,193},{2,194},{3,195},{4,196},{5,197},{6,198},{7,199},{8... | collective-permute-start | bytes 983048 | tf_op jit(solution)/shard_map/ppermute | solution.py:50
  21.5 18.3 %collective-permute-start.3 = (bf16[64,2560]{1,0:T(8,128)(2,1)S(1)}, bf16[64,2560]{1,0:T(8,128)(2,1)S(1)}, u32[]{:S(2)}, u32[]{:S(2)}) collective-permute-start(bf16[64,2560]{1,0:T(8,128)(2,1)S(1)} %collective-permute-done.refs_1_), channel_id=1, source_target_pairs={{0,1},{1,0},{2,3},{3,2},{4,5},{5,4},{6,7},{7,6},{8,9},{9,8},{10,11... | collective-permute-start | bytes 983048 | tf_op jit(solution)/shard_map/ppermute | solution.py:50
  25.4 14.4 %collective-permute-start.4 = (bf16[64,2560]{1,0:T(8,128)(2,1)S(1)}, bf16[64,2560]{1,0:T(8,128)(2,1)S(1)}, u32[]{:S(2)}, u32[]{:S(2)}) collective-permute-start(bf16[64,2560]{1,0:T(8,128)(2,1)S(1)} %collective-permute-done.1.refs_2_), channel_id=1, source_target_pairs={{0,1},{1,0},{2,3},{3,2},{4,5},{5,4},{6,7},{7,6},{8,9},{9,8},{10,11... | collective-permute-start | bytes 983048 | tf_op jit(solution)/shard_map/ppermute | solution.py:50
  31.9 8.0 %collective-permute-start.5 = (bf16[64,2560]{1,0:T(8,128)(2,1)S(1)}, bf16[64,2560]{1,0:T(8,128)(2,1)S(1)}, u32[]{:S(2)}, u32[]{:S(2)}) collective-permute-start(bf16[64,2560]{1,0:T(8,128)(2,1)S(1)} %collective-permute-done.2.refs_3_), channel_id=1, source_target_pairs={{0,1},{1,0},{2,3},{3,2},{4,5},{5,4},{6,7},{7,6},{8,9},{9,8},{10,11... | collective-permute-start | bytes 983048 | tf_op jit(solution)/shard_map/ppermute | solution.py:50
  32.4 15.3 %collective-permute-start.6 = (bf16[128,512]{1,0:T(8,128)(2,1)S(1)}, bf16[128,512]{1,0:T(8,128)(2,1)S(1)}, u32[]{:S(2)}, u32[]{:S(2)}) collective-permute-start(bf16[128,512]{1,0:T(8,128)(2,1)S(1)} %copy-done.15), channel_id=1, source_target_pairs={{0,0},{1,1},{2,64},{3,65},{4,128},{5,129},{6,192},{7,193},{8,8},{9... | collective-permute-start | bytes 393224 | tf_op jit(solution)/shard_map/ppermute | solution.py:50
  41.2 1.3 copy-start
  47.7 1.3 copy-start.1
  49.0 33.8 %all-to-all-start.1 = ((bf16[8,512,256]{2,1,0:T(8,128)(2,1)}), bf16[8,512,256]{2,1,0:T(8,128)(2,1)S(1)}, u32[]{:S(2)}, u32[]{:S(2)}) async-start(bf16[8,512,256]{2,1,0:T(8,128)(2,1)} %copy-done), calls=%async_computation.1 | async-start | bytes 4194304 | tf_op jit(solution)/shard_map/all_to_all | solution.py:293
  56.0 4.9 %copy-start.2 = (bf16[8,128,1024]{2,1,0:T(8,128)(2,1)S(1)}, bf16[8,128,1024]{2,1,0:T(8,128)(2,1)}, u32[]{:S(2)}) copy-start(bf16[8,128,1024]{2,1,0:T(8,128)(2,1)} %copy-done.1) | copy-start | bytes 6291460
  57.5 3.5 %collective-permute-start.7 = (bf16[8,128,512]{2,1,0:T(8,128)(2,1)S(1)}, bf16[8,128,512]{2,1,0:T(8,128)(2,1)S(1)}, u32[]{:S(2)}, u32[]{:S(2)}) collective-permute-start(bf16[8,128,512]{2,1,0:T(8,128)(2,1)S(1)} %slice.17), channel_id=1, source_target_pairs={{0,1},{1,0},{2,3},{3,2},{4,5},{5,4},{6,7},{7,6},{8,9},{9,8},{10,11... | collective-permute-start | bytes 3145736 | tf_op jit(solution)/shard_map/ppermute | solution.py:50
  62.3 14.4 %collective-permute-start.10 = (bf16[512,256]{1,0:T(8,128)(2,1)S(1)}, bf16[512,256]{1,0:T(8,128)(2,1)S(1)}, u32[]{:S(2)}, u32[]{:S(2)}) collective-permute-start(bf16[512,256]{1,0:T(8,128)(2,1)S(1)} %get-tuple-element.63), channel_id=1, source_target_pairs={{0,192},{1,193},{2,194},{3,195},{4,196},{5,197},{6,198},{7,199},{8... | collective-permute-start | bytes 786440 | tf_op jit(solution)/shard_map/ppermute | solution.py:50
  62.4 14.3 %collective-permute-start.8 = (bf16[512,256]{1,0:T(8,128)(2,1)S(1)}, bf16[512,256]{1,0:T(8,128)(2,1)S(1)}, u32[]{:S(2)}, u32[]{:S(2)}) collective-permute-start(bf16[512,256]{1,0:T(8,128)(2,1)S(1)} %get-tuple-element.61), channel_id=1, source_target_pairs={{0,64},{1,65},{2,66},{3,67},{4,68},{5,69},{6,70},{7,71},{8,72},{9,... | collective-permute-start | bytes 786440 | tf_op jit(solution)/shard_map/ppermute | solution.py:50
  65.0 11.7 %collective-permute-start.9 = (bf16[512,256]{1,0:T(8,128)(2,1)S(1)}, bf16[512,256]{1,0:T(8,128)(2,1)S(1)}, u32[]{:S(2)}, u32[]{:S(2)}) collective-permute-start(bf16[512,256]{1,0:T(8,128)(2,1)S(1)} %get-tuple-element.62), channel_id=1, source_target_pairs={{0,128},{1,129},{2,130},{3,131},{4,132},{5,133},{6,134},{7,135},{8... | collective-permute-start | bytes 786440 | tf_op jit(solution)/shard_map/ppermute | solution.py:50
  65.0 17.8 %collective-permute-start.11 = (bf16[128,512]{1,0:T(8,128)(2,1)S(1)}, bf16[128,512]{1,0:T(8,128)(2,1)S(1)}, u32[]{:S(2)}, u32[]{:S(2)}) collective-permute-start(bf16[128,512]{1,0:T(8,128)(2,1)S(1)} %collective-permute-done.6), channel_id=1, source_target_pairs={{0,32},{1,33},{2,34},{3,35},{4,36},{5,37},{6,38},{7,39},{8,40},{9,... | collective-permute-start | bytes 393224 | tf_op jit(solution)/shard_map/ppermute | solution.py:50
  77.5 0.8 copy-start.8
  82.9 36.3 %collective-permute-start.15 = (bf16[8,256,256]{2,1,0:T(8,128)(2,1)S(1)}, bf16[8,256,256]{2,1,0:T(8,128)(2,1)S(1)}, u32[]{:S(2)}, u32[]{:S(2)}) collective-permute-start(bf16[8,256,256]{2,1,0:T(8,128)(2,1)S(1)} %slice.18), channel_id=1, source_target_pairs={{0,1},{1,0},{2,3},{3,2},{4,5},{5,4},{6,7},{7,6},{8,9},{9,8},{10,11... | collective-permute-start | bytes 3145736 | tf_op jit(solution)/shard_map/ppermute | solution.py:50
  84.7 34.5 %collective-permute-start.12 = (bf16[2,128,512]{2,1,0:T(8,128)(2,1)S(1)}, bf16[2,128,512]{2,1,0:T(8,128)(2,1)S(1)}, u32[]{:S(2)}, u32[]{:S(2)}) collective-permute-start(bf16[2,128,512]{2,1,0:T(8,128)(2,1)S(1)} %pad_maximum_fusion.refs_0_), channel_id=1, source_target_pairs={{0,2},{1,3},{2,4},{3,5},{4,6},{5,7},{6,0},{7,1},{8,10},{9,11},{10,... | collective-permute-start | bytes 786440 | tf_op jit(solution)/shard_map/ppermute | solution.py:50
  84.8 34.4 %collective-permute-start.13 = (bf16[2,128,512]{2,1,0:T(8,128)(2,1)S(1)}, bf16[2,128,512]{2,1,0:T(8,128)(2,1)S(1)}, u32[]{:S(2)}, u32[]{:S(2)}) collective-permute-start(bf16[2,128,512]{2,1,0:T(8,128)(2,1)S(1)} %pad_maximum_fusion.refs_0_), channel_id=1, source_target_pairs={{0,4},{1,5},{2,6},{3,7},{4,0},{5,1},{6,2},{7,3},{8,12},{9,13},{10,... | collective-permute-start | bytes 786440 | tf_op jit(solution)/shard_map/ppermute | solution.py:50
  87.2 31.9 %collective-permute-start.14 = (bf16[2,128,512]{2,1,0:T(8,128)(2,1)S(1)}, bf16[2,128,512]{2,1,0:T(8,128)(2,1)S(1)}, u32[]{:S(2)}, u32[]{:S(2)}) collective-permute-start(bf16[2,128,512]{2,1,0:T(8,128)(2,1)S(1)} %pad_maximum_fusion.refs_0_), channel_id=1, source_target_pairs={{0,6},{1,7},{2,0},{3,1},{4,2},{5,3},{6,4},{7,5},{8,14},{9,15},{10,... | collective-permute-start | bytes 786440 | tf_op jit(solution)/shard_map/ppermute | solution.py:50
  91.5 27.7 %copy-start.9 = (f32[256,256]{1,0:T(8,128)}, f32[256,256]{1,0:T(8,128)S(1)}, u32[]{:S(2)}) copy-start(f32[256,256]{1,0:T(8,128)S(1)} %get-tuple-element.67) | copy-start | bytes 786436
  119.2 1.0 copy-start.6
  121.8 9.1 %copy-start.10 = (f32[256,256]{1,0:T(8,128)S(1)}, f32[256,256]{1,0:T(8,128)}, u32[]{:S(2)}) copy-start(f32[256,256]{1,0:T(8,128)} %copy-done.9) | copy-start | bytes 786436
  124.8 23.1 %collective-permute-start.16 = (bf16[256,512]{1,0:T(8,128)(2,1)S(1)}, bf16[256,512]{1,0:T(8,128)(2,1)S(1)}, u32[]{:S(2)}, u32[]{:S(2)}) collective-permute-start(bf16[256,512]{1,0:T(8,128)(2,1)S(1)} %get-tuple-element.100), channel_id=1, source_target_pairs={{0,0},{1,1},{2,64},{3,65},{4,128},{5,129},{6,192},{7,193},{8,8},{9... | collective-permute-start | bytes 786440 | tf_op jit(solution)/shard_map/ppermute | solution.py:50
  147.9 4.4 %collective-permute-start.20 = (bf16[256,256]{1,0:T(8,128)(2,1)S(1)}, bf16[256,256]{1,0:T(8,128)(2,1)S(1)}, u32[]{:S(2)}, u32[]{:S(2)}) collective-permute-start(bf16[256,256]{1,0:T(8,128)(2,1)S(1)} %get-tuple-element.84.w0), channel_id=1, source_target_pairs={{0,64},{1,65},{2,66},{3,67},{4,68},{5,69},{6,70},{7,71},{8,72},{9,... | collective-permute-start | bytes 393224 | tf_op jit(solution)/shard_map/ppermute | solution.py:50
  147.9 12.6 %collective-permute-start.17 = (bf16[256,512]{1,0:T(8,128)(2,1)S(1)}, bf16[256,512]{1,0:T(8,128)(2,1)}, u32[]{:S(2)}, u32[]{:S(2)}) collective-permute-start(bf16[256,512]{1,0:T(8,128)(2,1)S(1)} %collective-permute-done.16.refs_4_), channel_id=1, source_target_pairs={{0,8},{1,9},{2,10},{3,11},{4,12},{5,13},{6,14},{7,15},{8,16},{9,17... | collective-permute-start | bytes 786440 | tf_op jit(solution)/shard_map/ppermute | solution.py:50
  148.2 12.4 %collective-permute-start.18 = (bf16[256,512]{1,0:T(8,128)(2,1)S(1)}, bf16[256,512]{1,0:T(8,128)(2,1)}, u32[]{:S(2)}, u32[]{:S(2)}) collective-permute-start(bf16[256,512]{1,0:T(8,128)(2,1)S(1)} %collective-permute-done.16.refs_4_), channel_id=1, source_target_pairs={{0,16},{1,17},{2,18},{3,19},{4,20},{5,21},{6,22},{7,23},{8,24},{9,... | collective-permute-start | bytes 786440 | tf_op jit(solution)/shard_map/ppermute | solution.py:50
  150.9 12.7 %collective-permute-start.19 = (bf16[256,512]{1,0:T(8,128)(2,1)S(1)}, bf16[256,512]{1,0:T(8,128)(2,1)}, u32[]{:S(2)}, u32[]{:S(2)}) collective-permute-start(bf16[256,512]{1,0:T(8,128)(2,1)S(1)} %collective-permute-done.16.refs_4_), channel_id=1, source_target_pairs={{0,24},{1,25},{2,26},{3,27},{4,28},{5,29},{6,30},{7,31},{8,0},{9,1... | collective-permute-start | bytes 786440 | tf_op jit(solution)/shard_map/ppermute | solution.py:50
  151.1 5.4 %collective-permute-start.21 = (bf16[256,256]{1,0:T(8,128)(2,1)S(1)}, bf16[256,256]{1,0:T(8,128)(2,1)}, u32[]{:S(2)}, u32[]{:S(2)}) collective-permute-start(bf16[256,256]{1,0:T(8,128)(2,1)S(1)} %get-tuple-element.84.w0), channel_id=1, source_target_pairs={{0,128},{1,129},{2,130},{3,131},{4,132},{5,133},{6,134},{7,135},{8... | collective-permute-start | bytes 393224 | tf_op jit(solution)/shard_map/ppermute | solution.py:50
  152.3 0.7 copy-start.12
  153.0 7.5 %collective-permute-start.22 = (bf16[256,256]{1,0:T(8,128)(2,1)S(1)}, bf16[256,256]{1,0:T(8,128)(2,1)}, u32[]{:S(2)}, u32[]{:S(2)}) collective-permute-start(bf16[256,256]{1,0:T(8,128)(2,1)S(1)} %get-tuple-element.84.w0), channel_id=1, source_target_pairs={{0,192},{1,193},{2,194},{3,195},{4,196},{5,197},{6,198},{7,199},{8... | collective-permute-start | bytes 393224 | tf_op jit(solution)/shard_map/ppermute | solution.py:50
  153.3 12.8 %copy-start.7 = (bf16[8,256,256]{2,1,0:T(8,128)(2,1)S(1)}, bf16[8,256,256]{2,1,0:T(8,128)(2,1)}, u32[]{:S(2)}) copy-start(bf16[8,256,256]{2,1,0:T(8,128)(2,1)} %copy-done.6) | copy-start | bytes 3145732
  153.3 12.8 %copy-start.13 = (bf16[256,256]{1,0:T(8,128)(2,1)S(1)}, bf16[256,256]{1,0:T(8,128)(2,1)}, u32[]{:S(2)}) copy-start(bf16[256,256]{1,0:T(8,128)(2,1)} %copy-done.12) | copy-start | bytes 393220
  165.5 3.1 %collective-permute-start.23 = (bf16[512,1024]{1,0:T(8,128)(2,1)S(1)}, bf16[512,1024]{1,0:T(8,128)(2,1)S(1)}, u32[]{:S(2)}, u32[]{:S(2)}) collective-permute-start(bf16[512,1024]{1,0:T(8,128)(2,1)S(1)} %shard_map.185), channel_id=1, source_target_pairs={{0,1},{1,0},{2,3},{3,2},{4,5},{5,4},{6,7},{7,6},{8,9},{9,8},{10,11... | collective-permute-start | bytes 3145736 | tf_op jit(solution)/shard_map/ppermute | solution.py:50
  170.4 7.7 %collective-permute-start.24 = (bf16[128,1024]{1,0:T(8,128)(2,1)S(1)}, bf16[128,1024]{1,0:T(8,128)(2,1)S(1)}, u32[]{:S(2)}, u32[]{:S(2)}) collective-permute-start(bf16[128,1024]{1,0:T(8,128)(2,1)S(1)} %get-tuple-element.89), channel_id=1, source_target_pairs={{0,0},{1,32},{2,2},{3,34},{4,4},{5,36},{6,6},{7,38},{8,8},{9,40},{... | collective-permute-start | bytes 786440 | tf_op jit(solution)/shard_map/ppermute | solution.py:50
  178.1 23.6 %all-to-all-start.3 = ((bf16[8,128,256]{2,1,0:T(8,128)(2,1)}), bf16[8,128,256]{2,1,0:T(8,128)(2,1)S(1)}, u32[]{:S(2)}, u32[]{:S(2)}) async-start(bf16[8,128,256]{2,1,0:T(8,128)(2,1)} %shard_map.186), calls=%async_computation.3 | async-start | bytes 1048576 | tf_op jit(solution)/shard_map/all_to_all | solution.py:293
  182.9 12.3 %collective-permute-start.25 = (bf16[128,1024]{1,0:T(8,128)(2,1)S(1)}, bf16[128,1024]{1,0:T(8,128)(2,1)S(1)}, u32[]{:S(2)}, u32[]{:S(2)}) collective-permute-start(bf16[128,1024]{1,0:T(8,128)(2,1)S(1)} %get-tuple-element.93), channel_id=1, source_target_pairs={{0,64},{1,96},{2,66},{3,98},{4,68},{5,100},{6,70},{7,102},{8,72},{... | collective-permute-start | bytes 786440 | tf_op jit(solution)/shard_map/ppermute | solution.py:50
  185.1 13.8 %collective-permute-start.26 = (bf16[128,1024]{1,0:T(8,128)(2,1)S(1)}, bf16[128,1024]{1,0:T(8,128)(2,1)S(1)}, u32[]{:S(2)}, u32[]{:S(2)}) collective-permute-start(bf16[128,1024]{1,0:T(8,128)(2,1)S(1)} %get-tuple-element.94), channel_id=1, source_target_pairs={{0,128},{1,160},{2,130},{3,162},{4,132},{5,164},{6,134},{7,166},{8... | collective-permute-start | bytes 786440 | tf_op jit(solution)/shard_map/ppermute | solution.py:50
  187.4 13.4 %collective-permute-start.27 = (bf16[128,1024]{1,0:T(8,128)(2,1)S(1)}, bf16[128,1024]{1,0:T(8,128)(2,1)S(1)}, u32[]{:S(2)}, u32[]{:S(2)}) collective-permute-start(bf16[128,1024]{1,0:T(8,128)(2,1)S(1)} %get-tuple-element.95), channel_id=1, source_target_pairs={{0,192},{1,224},{2,194},{3,226},{4,196},{5,228},{6,198},{7,230},{8... | collective-permute-start | bytes 786440 | tf_op jit(solution)/shard_map/ppermute | solution.py:50

commit v2 on v1

--- a/solution.py
+++ b/solution.py
@@ -70,12 +70,8 @@
     return move(values, lambda x, z, y, h, c: (x, z + 1, y, h, c))
 
 
-def swap_xh(values):
-    return move(values, lambda x, z, y, h, c: (h, z, y, x, c))
-
-
-def move_home(values, k):
-    return move(values, lambda x, z, y, h, c: (x + k, c, y, h, z))
+def move_home(values):
+    return move(values, lambda x, z, y, h, c: (h, c, y, x, z))
 
 
 def adam_update(master, first_moment, second_moment, gradient, factor):
@@ -216,44 +212,60 @@
     return call(kernel, (shape((qd, ROWS)),) * NX, (own, other), flops=2**30)
 
 
-def sum_terms(terms, columns):
+def sum_terms(terms, columns, squares=None, copies=None):
     rows = terms[0].shape[-1]
 
     def kernel(*refs):
-        *term_refs, grad_ref, squares_ref = refs
+        *refs, grad_ref, squares_ref = refs
         total = None
-        for ref in term_refs:
-            parts = [ref[...]] if len(ref.shape) == 2 else [ref[i, :columns] for i in range(ref.shape[0])]
-            for part in parts:
-                part = part.astype(jnp.float32)
-                total = part if total is None else total + part
-        squares_ref[0, 0] = jnp.sum(total * total)
+        for ref in refs[: len(terms)]:
+            blocks = [ref[...]] if len(ref.shape) == 2 else [ref[i, :columns] for i in range(ref.shape[0])]
+            for block in blocks:
+                block = block.astype(jnp.float32)
+                total = block if total is None else total + block
+        if squares is None:
+            squares_ref[0, 0] = jnp.sum(total * total)
+        else:
+            both = refs[-1][0, 0] + jnp.sum(total * total)
+            squares_ref[...] = jnp.full(squares_ref.shape, both, jnp.float32)
         grad_ref[...] = total.T
 
+    squares_shape = shape((1, 1) if squares is None else (copies, 1, 128), jnp.float32)
     return pl.pallas_call(
         kernel,
-        out_shape=(shape((rows, columns), jnp.float32), shape((1, 1), jnp.float32)),
-        in_specs=[VMEM] * len(terms),
-        out_specs=(VMEM, SMEM),
+        out_shape=(shape((rows, columns), jnp.float32), squares_shape),
+        in_specs=[VMEM] * len(terms) + [SMEM] * (squares is not None),
+        out_specs=(VMEM, SMEM if squares is None else VMEM),
         compiler_params=pltpu.CompilerParams(vmem_limit_bytes=40 * 2**20),
         cost_estimate=pl.CostEstimate(flops=2**20, bytes_accessed=2**20, transcendentals=0),
-    )(*terms)
-
-
-def next_partial(place, which, context, weights, arrived=None):
+    )(*terms, *([] if squares is None else [squares]))
+
+
+def next_partial(place, which, context, context_z, weights, arrived=None):
     qd = context[0].shape[-1]
-    n_in = NH + NY
+    n_in = NX + 1 + len(weights)
 
     def kernel(place_ref, which_ref, *refs):
-        x, y, h = place_ref[0], place_ref[2], place_ref[3]
+        x, h = place_ref[0], place_ref[3]
         *refs, tokens_ref = refs
         outs = refs[n_in + (arrived is not None) :]
-        for j in range(NH):
-            tokens_ref[lax.rem(h - j - x + 2 * NX, NX)] = refs[j][which_ref[0]]
+
+        def take(blocks):
+            for j in range(NX):
+                tokens_ref[lax.rem(x - j - h + 2 * NX, NX)] = blocks[j]
+
+        @pl.when(which_ref[0] == 0)
+        def _():
+            take([ref[...] for ref in refs[:NX]])
+
+        @pl.when(which_ref[0] != 0)
+        def _():
+            take([refs[NX][j] for j in range(NX)])
+
         tokens = tokens_ref[...].reshape(NX * TOK, qd)
-        for j in range(NY):
-            cols = pl.ds(pl.multiple_of(lax.rem(y - j + NY, NY) * ROWS, ROWS), ROWS)
-            part = contract(tokens, refs[NH + j][...], 1, 1)
+        for j, weight_ref in enumerate(refs[NX + 1 : n_in]):
+            cols = slice(j * ROWS, (j + 1) * ROWS)
+            part = contract(tokens, weight_ref[...], 1, 1)
             if arrived is None:
                 outs[0][:, cols] = part.astype(jnp.bfloat16)
             else:
@@ -261,32 +273,55 @@
                 for k in range(NX):
                     outs[k][:, cols] = part[k * TOK : (k + 1) * TOK].astype(jnp.bfloat16)
 
+    width = len(weights) * ROWS
     if arrived is None:
-        out_shape = (shape((NX * TOK, NY * ROWS)),)
-        operands = (*context, *weights)
+        out_shape = (shape((NX * TOK, width)),)
+        operands = (*context, context_z, *weights)
     else:
-        out_shape = (shape((TOK, NY * ROWS)),) * NX
-        operands = (*context, *weights, arrived)
+        out_shape = (shape((TOK, width)),) * NX
+        operands = (*context, context_z, *weights, arrived)
     scratch = [pltpu.VMEM((NX, TOK, qd), jnp.bfloat16)]
-    return call(kernel, out_shape, operands, (place, which), 2**29, scratch)
-
-
-def keyvalue_partial(own, other, weights):
+    return call(kernel, out_shape, operands, (place, which), 2**28, scratch)
+
+
+def sum_homes(place, *chunks):
+    def kernel(place_ref, *refs):
+        *refs, out_ref = refs
+        y, j = place_ref[2], 0
+        for chunk in range(len(chunks)):
+            total = None
+            for ref in refs[chunk * NH : (chunk + 1) * NH]:
+                part = ref[...].astype(jnp.float32)
+                total = part if total is None else total + part
+            for m in range(total.shape[1] // ROWS):
+                cols = pl.ds(pl.multiple_of(lax.rem(y - j + NY, NY) * ROWS, ROWS), ROWS)
+                out_ref[:, cols] = total[:, m * ROWS : (m + 1) * ROWS].astype(jnp.bfloat16)
+                j += 1
+
+    operands = [part for chunk in chunks for part in chunk]
+    return call(kernel, shape((TOK, NY * ROWS)), operands, (place,))
+
+
+def keyvalue_partial(place, own, other, weights):
     kvw = weights[0].shape[1]
 
-    def kernel(own_ref, other_ref, w0, w1, w2, w3, out_ref):
-        for half, ref in enumerate((own_ref, other_ref)):
-            total = None
-            for j, weight in enumerate((w0, w1, w2, w3)):
-                first = ref.shape[1] - (NX - -j % NX) * HALF
-                block = ref[:, first : first + HALF].reshape(NZ * NY * HALF, ROWS)
-                part = contract(block, weight[...], 1, 0)
-                total = part if total is None else total + part
-            out_ref[:, half * HALF : (half + 1) * HALF] = total.astype(jnp.bfloat16).reshape(
-                NZ * NY, HALF, kvw
-            )
-
-    return call(kernel, shape((NZ * NY, TOK, kvw)), (own, other, *weights), flops=2**29)
+    def kernel(place_ref, own_ref, other_ref, w0, w1, w2, w3, *out_refs):
+        z, y = place_ref[1], place_ref[2]
+        for q, out_ref in enumerate(out_refs):
+            sets = [lax.rem(z + q, NZ) * NY + lax.rem(y + k, NY) for k in range(NY)]
+            for half, ref in enumerate((own_ref, other_ref)):
+                total = None
+                for j, weight in enumerate((w0, w1, w2, w3)):
+                    first = ref.shape[1] - (NX - -j % NX) * HALF
+                    block = jnp.concatenate([ref[i, first : first + HALF] for i in sets], axis=0)
+                    part = contract(block, weight[...], 1, 0)
+                    total = part if total is None else total + part
+                out_ref[:, half * HALF : (half + 1) * HALF] = total.astype(jnp.bfloat16).reshape(
+                    NY, HALF, kvw
+                )
+
+    out_shape = (shape((NY, TOK, kvw)),) * NZ
+    return call(kernel, out_shape, (own, other, *weights), (place,), 2**29)
 
 
 def to_set(values):
@@ -324,30 +359,21 @@
     place_kv, out_sent = after((place, out_sent))
     *kv_sent, kv_rest = kv_payload(place_kv, enc_states, kv_cotangent)
     kv_own = [kv_sent[0]] + [move_x(kv_sent[k], k) for k in range(1, NX)]
-    context = swap_xh(next_context)
     kv_other = [kv_rest] + [move_core(part) for part in kv_own[1:]]
 
     kv_part = kv_terms(place, kv_own, kv_other, next_states, kvw, kv_scale)
-    kv_part, out_landed, context = after((kv_part, out_landed, context))
+    kv_part, out_landed = after((kv_part, out_landed))
     kv_landed = to_set(kv_part)
     out_other = move_core(out_landed[:, :, : 2 * ROWS])
     out_parts = out_terms(out_landed, out_other, qd, out_scale)
-    context_z = move_z(context)
+    context = [next_context] + [move_x(next_context, j) for j in range(1, NX)]
     out_parts = [out_parts[0]] + [move_x(out_parts[k], k) for k in range(1, NX)]
     out_grad, out_squares = sum_terms(out_parts, qd)
-    kv_landed, out_squares, context_z = after((kv_landed, out_squares, context_z))
-    context = jnp.stack([context, context_z])
-    context = [context] + [move_h(context, j) for j in range(1, NH)]
-    kv_grad, kv_squares = sum_terms([kv_landed], kvw)
-    states_other = move_core(kv_landed[:, kvw:])
-
+    kv_landed, out_squares = after((kv_landed, out_squares))
     n_all = NX * NZ * NY * NH * NC
-    squares_all = lax.all_to_all(
-        jnp.broadcast_to((kv_squares + out_squares).reshape(1, 1, 1), (n_all, 1, 128)),
-        ("dp", "tensor"),
-        0,
-        0,
-    )
+    kv_grad, squares = sum_terms([kv_landed], kvw, out_squares, n_all)
+    states_other = move_core(kv_landed)
+    squares_all = lax.all_to_all(squares, ("dp", "tensor"), 0, 0)
     squares_all, context, states_other = after((squares_all, context, states_other))
     squares_total = jnp.sum(squares_all[:, 0, 0])
     factor = jnp.minimum(1.0, max_norm / (jnp.sqrt(squares_total) + 1e-06))
@@ -357,23 +383,22 @@
     new_kv_master, new_kv_first, new_kv_second = adam_update(
         kv_master, kv_first, kv_second, kv_grad, factor
     )
-
-    out_weight = swap_xh(new_out_master.astype(bf16))
-    out_weight, kv_weight = after((out_weight, new_kv_master.astype(bf16)))
+    out_weight, kv_weight = new_out_master.astype(bf16), new_kv_master.astype(bf16)
     out_weights = [out_weight] + [move_y(out_weight, j) for j in range(1, NY)]
     kv_weights = [kv_weight] + [move_x(kv_weight, j) for j in range(1, NX)]
     out_weights, kv_weights = after((out_weights, kv_weights))
-    (sent,) = next_partial(place, 1 - kept_half, context, out_weights)
+    context_z = move_z(jnp.stack(context))
+    (sent,) = next_partial(place, 1 - kept_half, context, context_z, out_weights)
     arrived = move_core(sent)
-    keyvalue = keyvalue_partial(kv_landed, states_other, kv_weights)
+    keyvalue = keyvalue_partial(place, kv_landed, states_other, kv_weights)
     arrived, keyvalue = after((arrived, keyvalue))
-    kept = next_partial(place, kept_half, context, out_weights, arrived)
-    homes = [move_home(block, k) for k, block in enumerate(kept)]
-    homes[0], keyvalue = after((homes[0], keyvalue))
-    next_output = sum(part.astype(f32) for part in homes).astype(bf16)
-
-    keyvalue = to_set(keyvalue)
-    keyvalue = jnp.sum(keyvalue.astype(f32), axis=0).astype(bf16)
+    kept = next_partial(place, kept_half, context, context_z, out_weights, arrived)
+    parts = [kept[0]] + [move_h(kept[k], k) for k in range(1, NH)]
+    next_output = move_home(sum_homes(place, parts))
+
+    keyvalue = (keyvalue[0].astype(f32) + move_z(keyvalue[1]).astype(f32)).astype(bf16)
+    keyvalue = [keyvalue[0]] + [move_y(keyvalue[k], k) for k in range(1, NY)]
+    keyvalue = sum(part.astype(f32) for part in keyvalue).astype(bf16)
     next_keyvalue = jnp.where(core == 0, keyvalue, jnp.roll(keyvalue, HALF, axis=0))
     return (
         new_kv_master,

time: 204 us -> 183 us (0.90)
  blocking collectives: 26.3 us -> 0 us
  waiting for transfers between devices: 76.3 us -> 86.1 us
  starting transfers between devices: 65.2 us -> 60.9 us
    all_to_all x1 -> x0, blocking collectives: 26.3 us -> none  [body(): lax.all_to_all(jnp.broadcast_to((kv_squares + out_squares).reshape(1, 1,...]
    all_to_all x0 -> x1, starting transfers between devices: none -> 12.9 us  [body(): squares_all = lax.all_to_all(squares, ('dp', 'tensor'), 0, 0)]
    ppermute x28 -> x30, starting transfers between devices: 47.5 us -> 36.9 us  [move(): return lax.ppermute(values, ('dp', 'tensor'), device_pairs(target))]
    ppermute x28 -> x30, waiting for transfers between devices: 76.3 us -> 85.7 us  [move(): return lax.ppermute(values, ('dp', 'tensor'), device_pairs(target))]
    all_to_all x3 -> x2, starting transfers between devices: 17.7 us -> 11 us  [to_set(): return lax.all_to_all(values, 'dp', 0, 0, axis_index_groups=ZY_GROUPS)]
    convert_element_type x3 -> x4, other arithmetic: 5.98 us -> 5.01 us  [the longest x1 2.95 us: body(): new_out_master.astype(bf16)]
    pallas_call x7 -> x8, Pallas kernels: 11.5 us -> 12.1 us  [call(): pl.pallas_call(kernel, out_shape=out_shape, in_specs=[SMEM] * len(scalars...]
    unnamed x32 -> x33, local copies, waits for them, and re-layouts: 9.22 us -> 9.63 us
  transfers between devices with their start and end apart: 31 -> 33, of which waited for: 15 -> 17; matrix products, arithmetic and copies ran while one was open for 2% -> 3% of each run, Pallas kernels for 4% -> 6%
where the time goes in v2:
time: 183 us; the launch traced here: 182 us
  waiting for transfers between devices  86.1 us (47%)
  starting transfers between devices  60.9 us (33%)
  Pallas kernels  14.6 us (8%)
  local copies, waits for them, and re-layouts  11.2 us (6%)
  other arithmetic  7.39 us (4%)
    ppermute x30, waiting for transfers between devices, move(): return lax.ppermute(values, ('dp', 'tensor'), device_pairs(target))  85.7 us
    ppermute x30, starting transfers between devices, move(): return lax.ppermute(values, ('dp', 'tensor'), device_pairs(target))  36.9 us
    all_to_all x1, starting transfers between devices, body(): squares_all = lax.all_to_all(squares, ('dp', 'tensor'), 0, 0)  12.9 us
    pallas_call x8, Pallas kernels, call(): pl.pallas_call(kernel, out_shape=out_shape, in_specs=[SMEM] * len(scalars...  12.1 us
    all_to_all x2, starting transfers between devices, to_set(): return lax.all_to_all(values, 'dp', 0, 0, axis_index_groups=ZY_GROUPS)  11 us
    unnamed x33, local copies, waits for them, and re-layouts  9.63 us
  transfers between devices with their start and end apart: 33, of which 17 were waited for; matrix products, arithmetic and copies ran while one was open for 3% of the time, Pallas kernels for 6%

profile of v2, /device:TPU:15, one launch (start us, length us, event | category | flops | bytes accessed | tf_op | source)
XLA Modules:
  0.0 181.8 jit_solution(5642678102569631150)
XLA Ops:
  0.8 1.6 copy-done.4
  3.3 2.1 %shard_map.179 = bf16[8,128,1024]{2,1,0:T(8,128)(2,1)} custom-call(s32[5]{0:T(128)S(1)} %stack.38.place_ref, bf16[128,8192]{1,0:T(8,128)(2,1)S(1)} %copy-done.4, bf16[128,512]{1,0:T(8,128)(2,1)S(1)} %copy-done.8), custom_call_target="tpu_custom_call" | custom-call | bytes 4325376 | tf_op jit(solution)/shard_map/pallas_call | solution.py:103
  5.4 5.8 %all-to-all-start = ((bf16[8,128,1024]{2,1,0:T(8,128)(2,1)}), bf16[8,128,1024]{2,1,0:T(8,128)(2,1)S(1)}, u32[]{:S(2)}, u32[]{:S(2)}) async-start(bf16[8,128,1024]{2,1,0:T(8,128)(2,1)} %shard_map.179), calls=%async_computation | async-start | bytes 4194304 | tf_op jit(solution)/shard_map/all_to_all | solution.py:328
  11.2 1.6 copy-done.3
  13.7 2.1 %collective-permute-start.1 = (bf16[64,2560]{1,0:T(8,128)(2,1)S(1)}, bf16[64,2560]{1,0:T(8,128)(2,1)S(1)}, u32[]{:S(2)}, u32[]{:S(2)}) collective-permute-start(bf16[64,2560]{1,0:T(8,128)(2,1)S(1)} %get-tuple-element.52), channel_id=1, source_target_pairs={{0,128},{1,129},{2,130},{3,131},{4,132},{5,133},{6,134},{7,135},{8... | collective-permute-start | bytes 983048 | tf_op jit(solution)/shard_map/ppermute | solution.py:50
  15.9 5.6 %collective-permute-done.refs_1_ = bf16[64,2560]{1,0:T(8,128)(2,1)S(1)} collective-permute-done((bf16[64,2560]{1,0:T(8,128)(2,1)S(1)}, bf16[64,2560]{1,0:T(8,128)(2,1)S(1)}, u32[]{:S(2)}, u32[]{:S(2)}) %collective-permute-start) | collective-permute-done | bytes 327712 | tf_op jit(solution)/shard_map/ppermute | solution.py:50
  21.5 3.9 %collective-permute-start.3 = (bf16[64,2560]{1,0:T(8,128)(2,1)S(1)}, bf16[64,2560]{1,0:T(8,128)(2,1)S(1)}, u32[]{:S(2)}, u32[]{:S(2)}) collective-permute-start(bf16[64,2560]{1,0:T(8,128)(2,1)S(1)} %collective-permute-done.refs_1_), channel_id=1, source_target_pairs={{0,1},{1,0},{2,3},{3,2},{4,5},{5,4},{6,7},{7,6},{8,9},{9,8},{10,11... | collective-permute-start | bytes 983048 | tf_op jit(solution)/shard_map/ppermute | solution.py:50
  25.4 2.0 %collective-permute-start.4 = (bf16[64,2560]{1,0:T(8,128)(2,1)S(1)}, bf16[64,2560]{1,0:T(8,128)(2,1)S(1)}, u32[]{:S(2)}, u32[]{:S(2)}) collective-permute-start(bf16[64,2560]{1,0:T(8,128)(2,1)S(1)} %collective-permute-done.1.refs_2_), channel_id=1, source_target_pairs={{0,1},{1,0},{2,3},{3,2},{4,5},{5,4},{6,7},{7,6},{8,9},{9,8},{10,11... | collective-permute-start | bytes 983048 | tf_op jit(solution)/shard_map/ppermute | solution.py:50
  27.5 4.4 %collective-permute-done.2.refs_3_ = bf16[64,2560]{1,0:T(8,128)(2,1)S(1)} collective-permute-done((bf16[64,2560]{1,0:T(8,128)(2,1)S(1)}, bf16[64,2560]{1,0:T(8,128)(2,1)S(1)}, u32[]{:S(2)}, u32[]{:S(2)}) %collective-permute-start.2) | collective-permute-done | bytes 327712 | tf_op jit(solution)/shard_map/ppermute | solution.py:50
  32.4 1.2 collective-permute-done.5.refs_7_
  33.6 1.3 shard_map.181
  35.0 1.3 copy-done
  36.3 1.4 copy-done.1
  37.7 5.1 %all-to-all-start.1 = ((bf16[8,512,256]{2,1,0:T(8,128)(2,1)}), bf16[8,512,256]{2,1,0:T(8,128)(2,1)S(1)}, u32[]{:S(2)}, u32[]{:S(2)}) async-start(bf16[8,512,256]{2,1,0:T(8,128)(2,1)} %copy-done), calls=%async_computation.1 | async-start | bytes 4194304 | tf_op jit(solution)/shard_map/all_to_all | solution.py:328
  42.8 1.4 slice.26
  45.3 2.3 %collective-permute-done.6.other_ref = bf16[8,128,512]{2,1,0:T(8,128)(2,1)S(1)} collective-permute-done((bf16[8,128,512]{2,1,0:T(8,128)(2,1)S(1)}, bf16[8,128,512]{2,1,0:T(8,128)(2,1)S(1)}, u32[]{:S(2)}, u32[]{:S(2)}) %collective-permute-start.6) | collective-permute-done | bytes 1048608 | tf_op jit(solution)/shard_map/ppermute | solution.py:50
  47.6 1.3 shard_map.182
  48.9 1.2 collective-permute-start.7
  50.1 1.3 collective-permute-start.8
  51.5 5.1 %collective-permute-done.7.refs_1_ = bf16[512,256]{1,0:T(8,128)(2,1)S(1)} collective-permute-done((bf16[512,256]{1,0:T(8,128)(2,1)S(1)}, bf16[512,256]{1,0:T(8,128)(2,1)S(1)}, u32[]{:S(2)}, u32[]{:S(2)}) %collective-permute-start.7) | collective-permute-done | bytes 262176 | tf_op jit(solution)/shard_map/ppermute | solution.py:50
  56.5 2.4 %collective-permute-done.8.refs_2_ = bf16[512,256]{1,0:T(8,128)(2,1)S(1)} collective-permute-done((bf16[512,256]{1,0:T(8,128)(2,1)S(1)}, bf16[512,256]{1,0:T(8,128)(2,1)S(1)}, u32[]{:S(2)}, u32[]{:S(2)}) %collective-permute-start.8) | collective-permute-done | bytes 262176 | tf_op jit(solution)/shard_map/ppermute | solution.py:50
  58.9 6.6 %collective-permute-done.9.refs_3_ = bf16[512,256]{1,0:T(8,128)(2,1)S(1)} collective-permute-done((bf16[512,256]{1,0:T(8,128)(2,1)S(1)}, bf16[512,256]{1,0:T(8,128)(2,1)S(1)}, u32[]{:S(2)}, u32[]{:S(2)}) %collective-permute-start.9) | collective-permute-done | bytes 262176 | tf_op jit(solution)/shard_map/ppermute | solution.py:50
  67.5 1.4 collective-permute-start.13
  68.9 1.6 shard_map.184
  70.6 12.9 %all-to-all-start.2 = ((f32[256,1,128]{2,1,0:T(1,128)}), f32[256,1,128]{2,1,0:T(1,128)S(1)}, u32[]{:S(2)}, u32[]{:S(2)}) async-start(f32[256,1,128]{2,1,0:T(1,128)} %get-tuple-element.65), calls=%async_computation.2 | async-start | bytes 262144 | tf_op jit(solution)/shard_map/all_to_all | solution.py:376
  83.9 2.1 %collective-permute-start.11 = (bf16[128,512]{1,0:T(8,128)(2,1)S(1)}, bf16[128,512]{1,0:T(8,128)(2,1)S(1)}, u32[]{:S(2)}, u32[]{:S(2)}) collective-permute-start(bf16[128,512]{1,0:T(8,128)(2,1)S(1)} %copy-done.6), channel_id=1, source_target_pairs={{0,128},{1,129},{2,130},{3,131},{4,132},{5,133},{6,134},{7,135},{8... | collective-permute-start | bytes 393224 | tf_op jit(solution)/shard_map/ppermute | solution.py:50
  86.0 3.0 %collective-permute-done.10.refs_1_ = bf16[128,512]{1,0:T(8,128)(2,1)S(1)} collective-permute-done((bf16[128,512]{1,0:T(8,128)(2,1)S(1)}, bf16[128,512]{1,0:T(8,128)(2,1)S(1)}, u32[]{:S(2)}, u32[]{:S(2)}) %collective-permute-start.10) | collective-permute-done | bytes 131104 | tf_op jit(solution)/shard_map/ppermute | solution.py:50
  89.0 1.7 collective-permute-done.11.refs_2_
  90.7 3.6 %collective-permute-done.12.refs_3_ = bf16[128,512]{1,0:T(8,128)(2,1)S(1)} collective-permute-done((bf16[128,512]{1,0:T(8,128)(2,1)S(1)}, bf16[128,512]{1,0:T(8,128)(2,1)S(1)}, u32[]{:S(2)}, u32[]{:S(2)}) %collective-permute-start.12) | collective-permute-done | bytes 131104 | tf_op jit(solution)/shard_map/ppermute | solution.py:50
  95.9 2.0 %fusion.5 = (bf16[256,256]{1,0:T(8,128)(2,1)S(1)}, f32[256,256]{1,0:T(8,128)}, f32[256,256]{1,0:T(8,128)}, f32[256,256]{1,0:T(8,128)}) fusion(f32[256,256]{1,0:T(8,128)S(1)} %copy-done.14, f32[256,256]{1,0:T(8,128)S(1)} %get-tuple-element.64, f32[]{:T(128)S(6)} %min_shard_map.3, f32[256,256]{1,0:T(8,128)S(1)} %copy-done.15, f32[256,256]{1,0:T(8,128)} %param.20), kind=kLoop, calls=%fused_computation.20 | loop fusion | flops 1114112 | bytes 1966084 | tf_op jit(solution)/shard_map/convert_element_type | solution.py:386
  97.9 1.4 collective-permute-start.18
  101.8 2.9 %fusion.7 = (bf16[256,512]{1,0:T(8,128)(2,1)S(1)}, f32[256,512]{1,0:T(8,128)}, f32[256,512]{1,0:T(8,128)}, f32[256,512]{1,0:T(8,128)}) fusion(f32[256,512]{1,0:T(8,128)} %param.21, f32[256,512]{1,0:T(8,128)} %copy-done.7, f32[]{:T(128)S(6)} %min_shard_map.3, f32[256,512]{1,0:T(8,128)} %param.22, f32[256,512]{1,0:T(8,128)} %param.23), kind=kLoop, calls=%fused_computation.21 | loop fusion | flops 2228224 | bytes 3932164 | tf_op jit(solution)/shard_map/convert_element_type | solution.py:386
  104.7 1.3 collective-permute-start.15
  107.7 1.7 collective-permute-start.17
  110.3 5.0 %collective-permute-done.20.w3 = bf16[256,256]{1,0:T(8,128)(2,1)} collective-permute-done((bf16[256,256]{1,0:T(8,128)(2,1)S(1)}, bf16[256,256]{1,0:T(8,128)(2,1)}, u32[]{:S(2)}, u32[]{:S(2)}) %collective-permute-start.20) | collective-permute-done | bytes 131104 | tf_op jit(solution)/shard_map/ppermute | solution.py:50
  115.3 6.0 %collective-permute-done.17.refs_8_ = bf16[256,512]{1,0:T(8,128)(2,1)} collective-permute-done((bf16[256,512]{1,0:T(8,128)(2,1)S(1)}, bf16[256,512]{1,0:T(8,128)(2,1)}, u32[]{:S(2)}, u32[]{:S(2)}) %collective-permute-start.17) | collective-permute-done | bytes 262176 | tf_op jit(solution)/shard_map/ppermute | solution.py:50
  121.3 1.9 %shard_map.185 = bf16[512,1024]{1,0:T(8,128)(2,1)S(1)} custom-call(s32[5]{0:T(128)S(1)} %stack.38.place_ref, s32[1]{0:T(128)S(6)} %sub.24.which_ref, bf16[128,512]{1,0:T(8,128)(2,1)S(1)} %copy-done.6, bf16[128,512]{1,0:T(8,128)(2,1)S(1)} %collective-permute-done.10.refs_1_, bf16[128,512]{1,0:T(8,128)(2,1)S(1)} %collective-permute-done.11.refs_2_, ...), custom_call_target="tpu_custom_call" | custom-call | flops 268435456 | bytes 3145728 | tf_op jit(solution)/shard_map/pallas_call | solution.py:103
  123.9 2.3 %shard_map.186 = (bf16[4,128,256]{2,1,0:T(8,128)(2,1)S(1)}, bf16[4,128,256]{2,1,0:T(8,128)(2,1)S(1)}) custom-call(s32[5]{0:T(128)S(1)} %stack.38.place_ref, bf16[8,512,256]{2,1,0:T(8,128)(2,1)S(1)} %all-to-all-done.1.refs_0_.own_ref, bf16[8,512,256]{2,1,0:T(8,128)(2,1)} %collective-permute-done.13.other_ref, bf16[256,256]{1,0:T(8,128)(2,1)S(1)} %get-tuple-element.77.w0, ...), custom_call_target="tpu_custom_call" | custom-call | flops 536870912 | bytes 5242880 | tf_op jit(solution)/shard_map/pallas_call | solution.py:103
  126.5 1.9 %shard_map.187 = (bf16[128,1024]{1,0:T(8,128)(2,1)S(1)}, bf16[128,1024]{1,0:T(8,128)(2,1)S(1)}, bf16[128,1024]{1,0:T(8,128)(2,1)S(1)}, bf16[128,1024]{1,0:T(8,128)(2,1)S(1)}) custom-call(s32[5]{0:T(128)S(1)} %stack.38.place_ref, s32[1]{0:T(128)} %bitcast.5.which_ref, bf16[128,512]{1,0:T(8,128)(2,1)S(1)} %copy-done.6, ...), custom_call_target="tpu_custom_call" | custom-call | flops 268435456 | bytes 4194304 | tf_op jit(solution)/shard_map/pallas_call | solution.py:103
  128.4 2.4 %collective-permute-start.26 = (bf16[128,1024]{1,0:T(8,128)(2,1)S(1)}, bf16[128,1024]{1,0:T(8,128)(2,1)S(1)}, u32[]{:S(2)}, u32[]{:S(2)}) collective-permute-start(bf16[128,1024]{1,0:T(8,128)(2,1)S(1)} %get-tuple-element.87), channel_id=1, source_target_pairs={{0,2},{1,3},{2,4},{3,5},{4,6},{5,7},{6,0},{7,1},{8,10},{9,11},{10,... | collective-permute-start | bytes 786440 | tf_op jit(solution)/shard_map/ppermute | solution.py:50
  130.8 3.5 %collective-permute-start.27 = (bf16[128,1024]{1,0:T(8,128)(2,1)S(1)}, bf16[128,1024]{1,0:T(8,128)(2,1)S(1)}, u32[]{:S(2)}, u32[]{:S(2)}) collective-permute-start(bf16[128,1024]{1,0:T(8,128)(2,1)S(1)} %get-tuple-element.88), channel_id=1, source_target_pairs={{0,4},{1,5},{2,6},{3,7},{4,0},{5,1},{6,2},{7,3},{8,12},{9,13},{10,... | collective-permute-start | bytes 786440 | tf_op jit(solution)/shard_map/ppermute | solution.py:50
  134.3 2.8 %collective-permute-start.28 = (bf16[128,1024]{1,0:T(8,128)(2,1)S(1)}, bf16[128,1024]{1,0:T(8,128)(2,1)S(1)}, u32[]{:S(2)}, u32[]{:S(2)}) collective-permute-start(bf16[128,1024]{1,0:T(8,128)(2,1)S(1)} %get-tuple-element.89), channel_id=1, source_target_pairs={{0,6},{1,7},{2,0},{3,1},{4,2},{5,3},{6,4},{7,5},{8,14},{9,15},{10,... | collective-permute-start | bytes 786440 | tf_op jit(solution)/shard_map/ppermute | solution.py:50
  137.8 1.2 collective-permute-start.24
  139.0 8.7 %collective-permute-done.26.refs_1_ = bf16[128,1024]{1,0:T(8,128)(2,1)S(1)} collective-permute-done((bf16[128,1024]{1,0:T(8,128)(2,1)S(1)}, bf16[128,1024]{1,0:T(8,128)(2,1)S(1)}, u32[]{:S(2)}, u32[]{:S(2)}) %collective-permute-start.26) | collective-permute-done | bytes 262176 | tf_op jit(solution)/shard_map/ppermute | solution.py:50
  147.7 8.5 %collective-permute-done.27.refs_2_ = bf16[128,1024]{1,0:T(8,128)(2,1)S(1)} collective-permute-done((bf16[128,1024]{1,0:T(8,128)(2,1)S(1)}, bf16[128,1024]{1,0:T(8,128)(2,1)S(1)}, u32[]{:S(2)}, u32[]{:S(2)}) %collective-permute-start.27) | collective-permute-done | bytes 262176 | tf_op jit(solution)/shard_map/ppermute | solution.py:50
  156.2 2.9 %collective-permute-done.28.refs_3_ = bf16[128,1024]{1,0:T(8,128)(2,1)S(1)} collective-permute-done((bf16[128,1024]{1,0:T(8,128)(2,1)S(1)}, bf16[128,1024]{1,0:T(8,128)(2,1)S(1)}, u32[]{:S(2)}, u32[]{:S(2)}) %collective-permute-start.28) | collective-permute-done | bytes 262176 | tf_op jit(solution)/shard_map/ppermute | solution.py:50
  159.7 1.9 %collective-permute-start.29 = (bf16[128,1024]{1,0:T(8,128)(2,1)S(1)}, bf16[128,1024]{1,0:T(8,128)(2,1)S(1)}, u32[]{:S(2)}, u32[]{:S(2)}) collective-permute-start(bf16[128,1024]{1,0:T(8,128)(2,1)S(1)} %shard_map.188), channel_id=1, source_target_pairs={{0,0},{1,32},{2,64},{3,96},{4,128},{5,160},{6,192},{7,224},{8,8},{... | collective-permute-start | bytes 786440 | tf_op jit(solution)/shard_map/ppermute | solution.py:50
  162.4 18.8 %collective-permute-done.29 = bf16[128,1024]{1,0:T(8,128)(2,1)S(1)} collective-permute-done((bf16[128,1024]{1,0:T(8,128)(2,1)S(1)}, bf16[128,1024]{1,0:T(8,128)(2,1)S(1)}, u32[]{:S(2)}, u32[]{:S(2)}) %collective-permute-start.29) | collective-permute-done | bytes 262176 | tf_op jit(solution)/shard_map/ppermute | solution.py:50
  (72 shorter events, 15.5 us)
Async XLA Ops:
  0.8 1.6 copy-start.4
  2.4 0.9 copy-start.8
  5.4 5.8 %copy-start.13 = (bf16[128,256]{1,0:T(8,128)(2,1)S(1)}, bf16[128,256]{1,0:T(8,128)(2,1)}, u32[]{:S(2)}) copy-start(bf16[128,256]{1,0:T(8,128)(2,1)} %cot_ref.3) | copy-start | bytes 196612
  5.4 31.0 %all-to-all-start = ((bf16[8,128,1024]{2,1,0:T(8,128)(2,1)}), bf16[8,128,1024]{2,1,0:T(8,128)(2,1)S(1)}, u32[]{:S(2)}, u32[]{:S(2)}) async-start(bf16[8,128,1024]{2,1,0:T(8,128)(2,1)} %shard_map.179), calls=%async_computation | async-start | bytes 4194304 | tf_op jit(solution)/shard_map/all_to_all | solution.py:328
  11.2 1.6 copy-start.3
  12.8 20.8 %copy-start.5 = (bf16[128,8192]{1,0:T(8,128)(2,1)S(1)}, bf16[128,8192]{1,0:T(8,128)(2,1)}, u32[]{:S(2)}) copy-start(bf16[128,8192]{1,0:T(8,128)(2,1)} %refs_8_.1) | copy-start | bytes 6291460
  13.5 8.0 %collective-permute-start = (bf16[64,2560]{1,0:T(8,128)(2,1)S(1)}, bf16[64,2560]{1,0:T(8,128)(2,1)S(1)}, u32[]{:S(2)}, u32[]{:S(2)}) collective-permute-start(bf16[64,2560]{1,0:T(8,128)(2,1)S(1)} %get-tuple-element.51), channel_id=1, source_target_pairs={{0,64},{1,65},{2,66},{3,67},{4,68},{5,69},{6,70},{7,71},{8,72},{9,... | collective-permute-start | bytes 983048 | tf_op jit(solution)/shard_map/ppermute | solution.py:50
  13.7 11.7 %collective-permute-start.1 = (bf16[64,2560]{1,0:T(8,128)(2,1)S(1)}, bf16[64,2560]{1,0:T(8,128)(2,1)S(1)}, u32[]{:S(2)}, u32[]{:S(2)}) collective-permute-start(bf16[64,2560]{1,0:T(8,128)(2,1)S(1)} %get-tuple-element.52), channel_id=1, source_target_pairs={{0,128},{1,129},{2,130},{3,131},{4,132},{5,133},{6,134},{7,135},{8... | collective-permute-start | bytes 983048 | tf_op jit(solution)/shard_map/ppermute | solution.py:50
  15.9 16.0 %collective-permute-start.2 = (bf16[64,2560]{1,0:T(8,128)(2,1)S(1)}, bf16[64,2560]{1,0:T(8,128)(2,1)S(1)}, u32[]{:S(2)}, u32[]{:S(2)}) collective-permute-start(bf16[64,2560]{1,0:T(8,128)(2,1)S(1)} %get-tuple-element.53), channel_id=1, source_target_pairs={{0,192},{1,193},{2,194},{3,195},{4,196},{5,197},{6,198},{7,199},{8... | collective-permute-start | bytes 983048 | tf_op jit(solution)/shard_map/ppermute | solution.py:50
  21.5 10.9 %collective-permute-start.3 = (bf16[64,2560]{1,0:T(8,128)(2,1)S(1)}, bf16[64,2560]{1,0:T(8,128)(2,1)S(1)}, u32[]{:S(2)}, u32[]{:S(2)}) collective-permute-start(bf16[64,2560]{1,0:T(8,128)(2,1)S(1)} %collective-permute-done.refs_1_), channel_id=1, source_target_pairs={{0,1},{1,0},{2,3},{3,2},{4,5},{5,4},{6,7},{7,6},{8,9},{9,8},{10,11... | collective-permute-start | bytes 983048 | tf_op jit(solution)/shard_map/ppermute | solution.py:50
  25.4 7.0 %collective-permute-start.4 = (bf16[64,2560]{1,0:T(8,128)(2,1)S(1)}, bf16[64,2560]{1,0:T(8,128)(2,1)S(1)}, u32[]{:S(2)}, u32[]{:S(2)}) collective-permute-start(bf16[64,2560]{1,0:T(8,128)(2,1)S(1)} %collective-permute-done.1.refs_2_), channel_id=1, source_target_pairs={{0,1},{1,0},{2,3},{3,2},{4,5},{5,4},{6,7},{7,6},{8,9},{9,8},{10,11... | collective-permute-start | bytes 983048 | tf_op jit(solution)/shard_map/ppermute | solution.py:50
  31.9 1.8 collective-permute-start.5
  35.0 1.4 copy-start
  36.3 1.4 copy-start.1
  37.7 29.8 %all-to-all-start.1 = ((bf16[8,512,256]{2,1,0:T(8,128)(2,1)}), bf16[8,512,256]{2,1,0:T(8,128)(2,1)S(1)}, u32[]{:S(2)}, u32[]{:S(2)}) async-start(bf16[8,512,256]{2,1,0:T(8,128)(2,1)} %copy-done), calls=%async_computation.1 | async-start | bytes 4194304 | tf_op jit(solution)/shard_map/all_to_all | solution.py:328
  42.8 4.8 %copy-start.2 = (bf16[8,128,1024]{2,1,0:T(8,128)(2,1)S(1)}, bf16[8,128,1024]{2,1,0:T(8,128)(2,1)}, u32[]{:S(2)}) copy-start(bf16[8,128,1024]{2,1,0:T(8,128)(2,1)} %copy-done.1) | copy-start | bytes 6291460
  44.3 3.3 %collective-permute-start.6 = (bf16[8,128,512]{2,1,0:T(8,128)(2,1)S(1)}, bf16[8,128,512]{2,1,0:T(8,128)(2,1)S(1)}, u32[]{:S(2)}, u32[]{:S(2)}) collective-permute-start(bf16[8,128,512]{2,1,0:T(8,128)(2,1)S(1)} %slice.26), channel_id=1, source_target_pairs={{0,1},{1,0},{2,3},{3,2},{4,5},{5,4},{6,7},{7,6},{8,9},{9,8},{10,11... | collective-permute-start | bytes 3145736 | tf_op jit(solution)/shard_map/ppermute | solution.py:50
  48.9 34.7 %copy-start.6 = (bf16[128,512]{1,0:T(8,128)(2,1)S(1)}, bf16[128,512]{1,0:T(8,128)(2,1)}, u32[]{:S(2)}) copy-start(bf16[128,512]{1,0:T(8,128)(2,1)} %refs_0_.1) | copy-start | bytes 393220
  48.9 47.0 %copy-start.14 = (f32[256,256]{1,0:T(8,128)S(1)}, f32[256,256]{1,0:T(8,128)}, u32[]{:S(2)}) copy-start(f32[256,256]{1,0:T(8,128)} %param.18) | copy-start | bytes 786436
  48.9 47.0 %copy-start.15 = (f32[256,256]{1,0:T(8,128)S(1)}, f32[256,256]{1,0:T(8,128)}, u32[]{:S(2)}) copy-start(f32[256,256]{1,0:T(8,128)} %param.19) | copy-start | bytes 786436
  48.9 7.6 %collective-permute-start.7 = (bf16[512,256]{1,0:T(8,128)(2,1)S(1)}, bf16[512,256]{1,0:T(8,128)(2,1)S(1)}, u32[]{:S(2)}, u32[]{:S(2)}) collective-permute-start(bf16[512,256]{1,0:T(8,128)(2,1)S(1)} %get-tuple-element.58), channel_id=1, source_target_pairs={{0,64},{1,65},{2,66},{3,67},{4,68},{5,69},{6,70},{7,71},{8,72},{9,... | collective-permute-start | bytes 786440 | tf_op jit(solution)/shard_map/ppermute | solution.py:50
  50.1 8.7 %collective-permute-start.8 = (bf16[512,256]{1,0:T(8,128)(2,1)S(1)}, bf16[512,256]{1,0:T(8,128)(2,1)S(1)}, u32[]{:S(2)}, u32[]{:S(2)}) collective-permute-start(bf16[512,256]{1,0:T(8,128)(2,1)S(1)} %get-tuple-element.59), channel_id=1, source_target_pairs={{0,128},{1,129},{2,130},{3,131},{4,132},{5,133},{6,134},{7,135},{8... | collective-permute-start | bytes 786440 | tf_op jit(solution)/shard_map/ppermute | solution.py:50
  51.5 14.0 %collective-permute-start.9 = (bf16[512,256]{1,0:T(8,128)(2,1)S(1)}, bf16[512,256]{1,0:T(8,128)(2,1)S(1)}, u32[]{:S(2)}, u32[]{:S(2)}) collective-permute-start(bf16[512,256]{1,0:T(8,128)(2,1)S(1)} %get-tuple-element.60), channel_id=1, source_target_pairs={{0,192},{1,193},{2,194},{3,195},{4,196},{5,197},{6,198},{7,199},{8... | collective-permute-start | bytes 786440 | tf_op jit(solution)/shard_map/ppermute | solution.py:50
  66.3 0.8 copy-start.7
  67.5 26.8 %collective-permute-start.13 = (bf16[8,512,256]{2,1,0:T(8,128)(2,1)S(1)}, bf16[8,512,256]{2,1,0:T(8,128)(2,1)}, u32[]{:S(2)}, u32[]{:S(2)}) collective-permute-start(bf16[8,512,256]{2,1,0:T(8,128)(2,1)S(1)} %all-to-all-done.1.refs_0_.own_ref), channel_id=1, source_target_pairs={{0,1},{1,0},{2,3},{3,2},{4,5},{5,4},{6,7},{7,6},{8,9},{9,8},{10,11... | collective-permute-start | bytes 6291464 | tf_op jit(solution)/shard_map/ppermute | solution.py:50
  70.6 23.7 %all-to-all-start.2 = ((f32[256,1,128]{2,1,0:T(1,128)}), f32[256,1,128]{2,1,0:T(1,128)S(1)}, u32[]{:S(2)}, u32[]{:S(2)}) async-start(f32[256,1,128]{2,1,0:T(1,128)} %get-tuple-element.65), calls=%async_computation.2 | async-start | bytes 262144 | tf_op jit(solution)/shard_map/all_to_all | solution.py:376
  83.5 5.5 %collective-permute-start.10 = (bf16[128,512]{1,0:T(8,128)(2,1)S(1)}, bf16[128,512]{1,0:T(8,128)(2,1)S(1)}, u32[]{:S(2)}, u32[]{:S(2)}) collective-permute-start(bf16[128,512]{1,0:T(8,128)(2,1)S(1)} %copy-done.6), channel_id=1, source_target_pairs={{0,64},{1,65},{2,66},{3,67},{4,68},{5,69},{6,70},{7,71},{8,72},{9,... | collective-permute-start | bytes 393224 | tf_op jit(solution)/shard_map/ppermute | solution.py:50
  83.9 6.8 %collective-permute-start.11 = (bf16[128,512]{1,0:T(8,128)(2,1)S(1)}, bf16[128,512]{1,0:T(8,128)(2,1)S(1)}, u32[]{:S(2)}, u32[]{:S(2)}) collective-permute-start(bf16[128,512]{1,0:T(8,128)(2,1)S(1)} %copy-done.6), channel_id=1, source_target_pairs={{0,128},{1,129},{2,130},{3,131},{4,132},{5,133},{6,134},{7,135},{8... | collective-permute-start | bytes 393224 | tf_op jit(solution)/shard_map/ppermute | solution.py:50
  86.0 8.3 %collective-permute-start.12 = (bf16[128,512]{1,0:T(8,128)(2,1)S(1)}, bf16[128,512]{1,0:T(8,128)(2,1)S(1)}, u32[]{:S(2)}, u32[]{:S(2)}) collective-permute-start(bf16[128,512]{1,0:T(8,128)(2,1)S(1)} %copy-done.6), channel_id=1, source_target_pairs={{0,192},{1,193},{2,194},{3,195},{4,196},{5,197},{6,198},{7,199},{8... | collective-permute-start | bytes 393224 | tf_op jit(solution)/shard_map/ppermute | solution.py:50
  97.9 9.2 %collective-permute-start.18 = (bf16[256,256]{1,0:T(8,128)(2,1)S(1)}, bf16[256,256]{1,0:T(8,128)(2,1)S(1)}, u32[]{:S(2)}, u32[]{:S(2)}) collective-permute-start(bf16[256,256]{1,0:T(8,128)(2,1)S(1)} %get-tuple-element.77.w0), channel_id=1, source_target_pairs={{0,64},{1,65},{2,66},{3,67},{4,68},{5,69},{6,70},{7,71},{8,72},{9,... | collective-permute-start | bytes 393224 | tf_op jit(solution)/shard_map/ppermute | solution.py:50
  99.3 10.1 %collective-permute-start.19 = (bf16[256,256]{1,0:T(8,128)(2,1)S(1)}, bf16[256,256]{1,0:T(8,128)(2,1)S(1)}, u32[]{:S(2)}, u32[]{:S(2)}) collective-permute-start(bf16[256,256]{1,0:T(8,128)(2,1)S(1)} %get-tuple-element.77.w0), channel_id=1, source_target_pairs={{0,128},{1,129},{2,130},{3,131},{4,132},{5,133},{6,134},{7,135},{8... | collective-permute-start | bytes 393224 | tf_op jit(solution)/shard_map/ppermute | solution.py:50
  100.5 20.8 %collective-permute-start.14 = (bf16[4,128,512]{2,1,0:T(8,128)(2,1)}, bf16[4,128,512]{2,1,0:T(8,128)(2,1)S(1)}, u32[]{:S(2)}, u32[]{:S(2)}) collective-permute-start(bf16[4,128,512]{2,1,0:T(8,128)(2,1)} %pad_maximum_fusion), channel_id=1, source_target_pairs={{0,32},{1,33},{2,34},{3,35},{4,36},{5,37},{6,38},{7,39},{8,40},{9,... | collective-permute-start | bytes 1572872 | tf_op jit(solution)/shard_map/ppermute | solution.py:50
  104.7 10.6 %collective-permute-start.15 = (bf16[256,512]{1,0:T(8,128)(2,1)S(1)}, bf16[256,512]{1,0:T(8,128)(2,1)}, u32[]{:S(2)}, u32[]{:S(2)}) collective-permute-start(bf16[256,512]{1,0:T(8,128)(2,1)S(1)} %get-tuple-element.72.refs_5_), channel_id=1, source_target_pairs={{0,8},{1,9},{2,10},{3,11},{4,12},{5,13},{6,14},{7,15},{8,16},{9,17... | collective-permute-start | bytes 786440 | tf_op jit(solution)/shard_map/ppermute | solution.py:50
  106.0 9.3 %collective-permute-start.16 = (bf16[256,512]{1,0:T(8,128)(2,1)S(1)}, bf16[256,512]{1,0:T(8,128)(2,1)}, u32[]{:S(2)}, u32[]{:S(2)}) collective-permute-start(bf16[256,512]{1,0:T(8,128)(2,1)S(1)} %get-tuple-element.72.refs_5_), channel_id=1, source_target_pairs={{0,16},{1,17},{2,18},{3,19},{4,20},{5,21},{6,22},{7,23},{8,24},{9,... | collective-permute-start | bytes 786440 | tf_op jit(solution)/shard_map/ppermute | solution.py:50
  107.1 0.7 copy-start.9
  107.7 13.6 %collective-permute-start.17 = (bf16[256,512]{1,0:T(8,128)(2,1)S(1)}, bf16[256,512]{1,0:T(8,128)(2,1)}, u32[]{:S(2)}, u32[]{:S(2)}) collective-permute-start(bf16[256,512]{1,0:T(8,128)(2,1)S(1)} %get-tuple-element.72.refs_5_), channel_id=1, source_target_pairs={{0,24},{1,25},{2,26},{3,27},{4,28},{5,29},{6,30},{7,31},{8,0},{9,1... | collective-permute-start | bytes 786440 | tf_op jit(solution)/shard_map/ppermute | solution.py:50
  110.0 5.3 %collective-permute-start.20 = (bf16[256,256]{1,0:T(8,128)(2,1)S(1)}, bf16[256,256]{1,0:T(8,128)(2,1)}, u32[]{:S(2)}, u32[]{:S(2)}) collective-permute-start(bf16[256,256]{1,0:T(8,128)(2,1)S(1)} %get-tuple-element.77.w0), channel_id=1, source_target_pairs={{0,192},{1,193},{2,194},{3,195},{4,196},{5,197},{6,198},{7,199},{8... | collective-permute-start | bytes 393224 | tf_op jit(solution)/shard_map/ppermute | solution.py:50
  110.3 13.6 %copy-start.10 = (bf16[256,256]{1,0:T(8,128)(2,1)S(1)}, bf16[256,256]{1,0:T(8,128)(2,1)}, u32[]{:S(2)}) copy-start(bf16[256,256]{1,0:T(8,128)(2,1)} %copy-done.9) | copy-start | bytes 393220
  110.3 13.6 %copy-start.12 = (bf16[256,256]{1,0:T(8,128)(2,1)S(1)}, bf16[256,256]{1,0:T(8,128)(2,1)}, u32[]{:S(2)}) copy-start(bf16[256,256]{1,0:T(8,128)(2,1)} %copy-done.11) | copy-start | bytes 393220
  123.3 3.0 %collective-permute-start.21 = (bf16[512,1024]{1,0:T(8,128)(2,1)S(1)}, bf16[512,1024]{1,0:T(8,128)(2,1)S(1)}, u32[]{:S(2)}, u32[]{:S(2)}) collective-permute-start(bf16[512,1024]{1,0:T(8,128)(2,1)S(1)} %shard_map.185), channel_id=1, source_target_pairs={{0,1},{1,0},{2,3},{3,2},{4,5},{5,4},{6,7},{7,6},{8,9},{9,8},{10,11... | collective-permute-start | bytes 3145736 | tf_op jit(solution)/shard_map/ppermute | solution.py:50
  126.3 10.9 %collective-permute-start.22 = (bf16[4,128,256]{2,1,0:T(8,128)(2,1)S(1)}, bf16[4,128,256]{2,1,0:T(8,128)(2,1)S(1)}, u32[]{:S(2)}, u32[]{:S(2)}) collective-permute-start(bf16[4,128,256]{2,1,0:T(8,128)(2,1)S(1)} %get-tuple-element.84), channel_id=1, source_target_pairs={{0,32},{1,33},{2,34},{3,35},{4,36},{5,37},{6,38},{7,39},{8,40},{9,... | collective-permute-start | bytes 786440 | tf_op jit(solution)/shard_map/ppermute | solution.py:50
  128.4 19.2 %collective-permute-start.26 = (bf16[128,1024]{1,0:T(8,128)(2,1)S(1)}, bf16[128,1024]{1,0:T(8,128)(2,1)S(1)}, u32[]{:S(2)}, u32[]{:S(2)}) collective-permute-start(bf16[128,1024]{1,0:T(8,128)(2,1)S(1)} %get-tuple-element.87), channel_id=1, source_target_pairs={{0,2},{1,3},{2,4},{3,5},{4,6},{5,7},{6,0},{7,1},{8,10},{9,11},{10,... | collective-permute-start | bytes 786440 | tf_op jit(solution)/shard_map/ppermute | solution.py:50
  130.8 25.3 %collective-permute-start.27 = (bf16[128,1024]{1,0:T(8,128)(2,1)S(1)}, bf16[128,1024]{1,0:T(8,128)(2,1)S(1)}, u32[]{:S(2)}, u32[]{:S(2)}) collective-permute-start(bf16[128,1024]{1,0:T(8,128)(2,1)S(1)} %get-tuple-element.88), channel_id=1, source_target_pairs={{0,4},{1,5},{2,6},{3,7},{4,0},{5,1},{6,2},{7,3},{8,12},{9,13},{10,... | collective-permute-start | bytes 786440 | tf_op jit(solution)/shard_map/ppermute | solution.py:50
  134.3 24.7 %collective-permute-start.28 = (bf16[128,1024]{1,0:T(8,128)(2,1)S(1)}, bf16[128,1024]{1,0:T(8,128)(2,1)S(1)}, u32[]{:S(2)}, u32[]{:S(2)}) collective-permute-start(bf16[128,1024]{1,0:T(8,128)(2,1)S(1)} %get-tuple-element.89), channel_id=1, source_target_pairs={{0,6},{1,7},{2,0},{3,1},{4,2},{5,3},{6,4},{7,5},{8,14},{9,15},{10,... | collective-permute-start | bytes 786440 | tf_op jit(solution)/shard_map/ppermute | solution.py:50
  137.3 24.4 %collective-permute-start.23 = (bf16[128,256]{1,0:T(8,128)(2,1)S(1)}, bf16[128,256]{1,0:T(8,128)(2,1)S(1)}, u32[]{:S(2)}, u32[]{:S(2)}) collective-permute-start(bf16[128,256]{1,0:T(8,128)(2,1)S(1)} %get-tuple-element.98), channel_id=1, source_target_pairs={{0,8},{1,9},{2,10},{3,11},{4,12},{5,13},{6,14},{7,15},{8,16},{9,17... | collective-permute-start | bytes 196616 | tf_op jit(solution)/shard_map/ppermute | solution.py:50
  137.8 23.9 %collective-permute-start.24 = (bf16[128,256]{1,0:T(8,128)(2,1)S(1)}, bf16[128,256]{1,0:T(8,128)(2,1)S(1)}, u32[]{:S(2)}, u32[]{:S(2)}) collective-permute-start(bf16[128,256]{1,0:T(8,128)(2,1)S(1)} %get-tuple-element.100), channel_id=1, source_target_pairs={{0,16},{1,17},{2,18},{3,19},{4,20},{5,21},{6,22},{7,23},{8,24},{9,... | collective-permute-start | bytes 196616 | tf_op jit(solution)/shard_map/ppermute | solution.py:50
  147.7 14.0 %collective-permute-start.25 = (bf16[128,256]{1,0:T(8,128)(2,1)S(1)}, bf16[128,256]{1,0:T(8,128)(2,1)S(1)}, u32[]{:S(2)}, u32[]{:S(2)}) collective-permute-start(bf16[128,256]{1,0:T(8,128)(2,1)S(1)} %get-tuple-element.99), channel_id=1, source_target_pairs={{0,24},{1,25},{2,26},{3,27},{4,28},{5,29},{6,30},{7,31},{8,0},{9,1... | collective-permute-start | bytes 196616 | tf_op jit(solution)/shard_map/ppermute | solution.py:50
  159.7 21.4 %collective-permute-start.29 = (bf16[128,1024]{1,0:T(8,128)(2,1)S(1)}, bf16[128,1024]{1,0:T(8,128)(2,1)S(1)}, u32[]{:S(2)}, u32[]{:S(2)}) collective-permute-start(bf16[128,1024]{1,0:T(8,128)(2,1)S(1)} %shard_map.188), channel_id=1, source_target_pairs={{0,0},{1,32},{2,64},{3,96},{4,128},{5,160},{6,192},{7,224},{8,8},{... | collective-permute-start | bytes 786440 | tf_op jit(solution)/shard_map/ppermute | solution.py:50
  (1 other events, 0.7 us)

commit v3 on v2

--- a/solution.py
+++ b/solution.py
@@ -377,13 +377,11 @@
     squares_all, context, states_other = after((squares_all, context, states_other))
     squares_total = jnp.sum(squares_all[:, 0, 0])
     factor = jnp.minimum(1.0, max_norm / (jnp.sqrt(squares_total) + 1e-06))
-    new_out_master, new_out_first, new_out_second = adam_update(
-        out_master, out_first, out_second, out_grad, factor
-    )
+    out_weight = adam_update(out_master, out_first, out_second, out_grad, factor)[0].astype(bf16)
     new_kv_master, new_kv_first, new_kv_second = adam_update(
         kv_master, kv_first, kv_second, kv_grad, factor
     )
-    out_weight, kv_weight = new_out_master.astype(bf16), new_kv_master.astype(bf16)
+    kv_weight = new_kv_master.astype(bf16)
     out_weights = [out_weight] + [move_y(out_weight, j) for j in range(1, NY)]
     kv_weights = [kv_weight] + [move_x(kv_weight, j) for j in range(1, NX)]
     out_weights, kv_weights = after((out_weights, kv_weights))
@@ -395,6 +393,10 @@
     kept = next_partial(place, kept_half, context, context_z, out_weights, arrived)
     parts = [kept[0]] + [move_h(kept[k], k) for k in range(1, NH)]
     next_output = move_home(sum_homes(place, parts))
+    out_grad, factor, _ = after((out_grad, factor, kept[0]))
+    new_out_master, new_out_first, new_out_second = adam_update(
+        out_master, out_first, out_second, out_grad, factor
+    )
 
     keyvalue = (keyvalue[0].astype(f32) + move_z(keyvalue[1]).astype(f32)).astype(bf16)
     keyvalue = [keyvalue[0]] + [move_y(keyvalue[k], k) for k in range(1, NY)]

time: 183 us -> 190 us (1.038)
  local copies, waits for them, and re-layouts: 11.2 us -> 18.7 us
  waiting for transfers between devices: 86.1 us -> 83.1 us
    unnamed x33 -> x65, local copies, waits for them, and re-layouts: 9.63 us -> 17.2 us
    ppermute x30, waiting for transfers between devices: 85.7 us -> 81.9 us  [move(): return lax.ppermute(values, ('dp', 'tensor'), device_pairs(target))]
    convert_element_type x2, other arithmetic: 4.91 us -> 2.71 us  [the longest x1 2.27 us: body(): kv_weight = new_kv_master.astype(bf16)]
  transfers between devices with their start and end apart: 33 -> 33, of which waited for: 17 -> 16; matrix products, arithmetic and copies ran while one was open for 3% -> 3% of each run, Pallas kernels for 6% -> 6%
where the time goes in v3:
time: 190 us; the launch traced here: 189 us
  waiting for transfers between devices  83.1 us (44%)
  starting transfers between devices  62.4 us (33%)
  local copies, waits for them, and re-layouts  18.7 us (10%)
  Pallas kernels  15.5 us (8%)
  other arithmetic  7.58 us (4%)
    ppermute x30, waiting for transfers between devices, move(): return lax.ppermute(values, ('dp', 'tensor'), device_pairs(target))  81.9 us
    ppermute x30, starting transfers between devices, move(): return lax.ppermute(values, ('dp', 'tensor'), device_pairs(target))  38.4 us
    unnamed x65, local copies, waits for them, and re-layouts  17.2 us
    pallas_call x8, Pallas kernels, call(): pl.pallas_call(kernel, out_shape=out_shape, in_specs=[SMEM] * len(scalars...  13.1 us
    all_to_all x1, starting transfers between devices, body(): squares_all = lax.all_to_all(squares, ('dp', 'tensor'), 0, 0)  12.9 us
    all_to_all x2, starting transfers between devices, to_set(): return lax.all_to_all(values, 'dp', 0, 0, axis_index_groups=ZY_GROUPS)  11 us
  transfers between devices with their start and end apart: 33, of which 16 were waited for; matrix products, arithmetic and copies ran while one was open for 3% of the time, Pallas kernels for 6%

profile of v3, /device:TPU:15, one launch (start us, length us, event | category | flops | bytes accessed | tf_op | source)
XLA Modules:
  0.0 189.0 jit_solution(13595344741553824156)
XLA Ops:
  0.8 1.6 copy-done.4
  3.3 2.1 %shard_map.179 = bf16[8,128,1024]{2,1,0:T(8,128)(2,1)} custom-call(s32[5]{0:T(128)S(1)} %stack.38.place_ref, bf16[128,8192]{1,0:T(8,128)(2,1)S(1)} %copy-done.4, bf16[128,512]{1,0:T(8,128)(2,1)S(1)} %copy-done.20), custom_call_target="tpu_custom_call" | custom-call | bytes 4325376 | tf_op jit(solution)/shard_map/pallas_call | solution.py:103
  5.4 5.8 %all-to-all-start = ((bf16[8,128,1024]{2,1,0:T(8,128)(2,1)}), bf16[8,128,1024]{2,1,0:T(8,128)(2,1)S(1)}, u32[]{:S(2)}, u32[]{:S(2)}) async-start(bf16[8,128,1024]{2,1,0:T(8,128)(2,1)} %shard_map.179), calls=%async_computation | async-start | bytes 4194304 | tf_op jit(solution)/shard_map/all_to_all | solution.py:328
  11.2 1.6 copy-done.3
  13.7 2.1 %collective-permute-start.1 = (bf16[64,2560]{1,0:T(8,128)(2,1)S(1)}, bf16[64,2560]{1,0:T(8,128)(2,1)S(1)}, u32[]{:S(2)}, u32[]{:S(2)}) collective-permute-start(bf16[64,2560]{1,0:T(8,128)(2,1)S(1)} %get-tuple-element.54), channel_id=1, source_target_pairs={{0,128},{1,129},{2,130},{3,131},{4,132},{5,133},{6,134},{7,135},{8... | collective-permute-start | bytes 983048 | tf_op jit(solution)/shard_map/ppermute | solution.py:50
  15.9 5.6 %collective-permute-done.refs_1_ = bf16[64,2560]{1,0:T(8,128)(2,1)S(1)} collective-permute-done((bf16[64,2560]{1,0:T(8,128)(2,1)S(1)}, bf16[64,2560]{1,0:T(8,128)(2,1)S(1)}, u32[]{:S(2)}, u32[]{:S(2)}) %collective-permute-start) | collective-permute-done | bytes 327712 | tf_op jit(solution)/shard_map/ppermute | solution.py:50
  21.5 3.9 %collective-permute-start.3 = (bf16[64,2560]{1,0:T(8,128)(2,1)S(1)}, bf16[64,2560]{1,0:T(8,128)(2,1)S(1)}, u32[]{:S(2)}, u32[]{:S(2)}) collective-permute-start(bf16[64,2560]{1,0:T(8,128)(2,1)S(1)} %collective-permute-done.refs_1_), channel_id=1, source_target_pairs={{0,1},{1,0},{2,3},{3,2},{4,5},{5,4},{6,7},{7,6},{8,9},{9,8},{10,11... | collective-permute-start | bytes 983048 | tf_op jit(solution)/shard_map/ppermute | solution.py:50
  25.4 2.0 %collective-permute-start.4 = (bf16[64,2560]{1,0:T(8,128)(2,1)S(1)}, bf16[64,2560]{1,0:T(8,128)(2,1)S(1)}, u32[]{:S(2)}, u32[]{:S(2)}) collective-permute-start(bf16[64,2560]{1,0:T(8,128)(2,1)S(1)} %collective-permute-done.1.refs_2_), channel_id=1, source_target_pairs={{0,1},{1,0},{2,3},{3,2},{4,5},{5,4},{6,7},{7,6},{8,9},{9,8},{10,11... | collective-permute-start | bytes 983048 | tf_op jit(solution)/shard_map/ppermute | solution.py:50
  27.4 4.4 %collective-permute-done.2.refs_3_ = bf16[64,2560]{1,0:T(8,128)(2,1)S(1)} collective-permute-done((bf16[64,2560]{1,0:T(8,128)(2,1)S(1)}, bf16[64,2560]{1,0:T(8,128)(2,1)S(1)}, u32[]{:S(2)}, u32[]{:S(2)}) %collective-permute-start.2) | collective-permute-done | bytes 327712 | tf_op jit(solution)/shard_map/ppermute | solution.py:50
  32.4 1.2 collective-permute-done.5.refs_7_
  33.6 1.3 shard_map.181
  35.0 1.3 copy-done
  36.3 1.3 copy-done.1
  37.6 5.1 %all-to-all-start.1 = ((bf16[8,512,256]{2,1,0:T(8,128)(2,1)}), bf16[8,512,256]{2,1,0:T(8,128)(2,1)S(1)}, u32[]{:S(2)}, u32[]{:S(2)}) async-start(bf16[8,512,256]{2,1,0:T(8,128)(2,1)} %copy-done), calls=%async_computation.1 | async-start | bytes 4194304 | tf_op jit(solution)/shard_map/all_to_all | solution.py:328
  42.8 1.4 slice.26
  45.2 2.3 %collective-permute-done.6.other_ref = bf16[8,128,512]{2,1,0:T(8,128)(2,1)S(1)} collective-permute-done((bf16[8,128,512]{2,1,0:T(8,128)(2,1)S(1)}, bf16[8,128,512]{2,1,0:T(8,128)(2,1)S(1)}, u32[]{:S(2)}, u32[]{:S(2)}) %collective-permute-start.6) | collective-permute-done | bytes 1048608 | tf_op jit(solution)/shard_map/ppermute | solution.py:50
  47.5 1.3 shard_map.182
  48.8 1.2 collective-permute-start.7
  50.1 1.3 collective-permute-start.8
  51.4 5.1 %collective-permute-done.7.refs_1_ = bf16[512,256]{1,0:T(8,128)(2,1)S(1)} collective-permute-done((bf16[512,256]{1,0:T(8,128)(2,1)S(1)}, bf16[512,256]{1,0:T(8,128)(2,1)S(1)}, u32[]{:S(2)}, u32[]{:S(2)}) %collective-permute-start.7) | collective-permute-done | bytes 262176 | tf_op jit(solution)/shard_map/ppermute | solution.py:50
  56.4 2.4 %collective-permute-done.8.refs_2_ = bf16[512,256]{1,0:T(8,128)(2,1)S(1)} collective-permute-done((bf16[512,256]{1,0:T(8,128)(2,1)S(1)}, bf16[512,256]{1,0:T(8,128)(2,1)S(1)}, u32[]{:S(2)}, u32[]{:S(2)}) %collective-permute-start.8) | collective-permute-done | bytes 262176 | tf_op jit(solution)/shard_map/ppermute | solution.py:50
  58.8 6.6 %collective-permute-done.9.refs_3_ = bf16[512,256]{1,0:T(8,128)(2,1)S(1)} collective-permute-done((bf16[512,256]{1,0:T(8,128)(2,1)S(1)}, bf16[512,256]{1,0:T(8,128)(2,1)S(1)}, u32[]{:S(2)}, u32[]{:S(2)}) %collective-permute-start.9) | collective-permute-done | bytes 262176 | tf_op jit(solution)/shard_map/ppermute | solution.py:50
  67.5 1.4 collective-permute-start.13
  68.9 1.6 shard_map.184
  70.5 12.9 %all-to-all-start.2 = ((f32[256,1,128]{2,1,0:T(1,128)}), f32[256,1,128]{2,1,0:T(1,128)S(1)}, u32[]{:S(2)}, u32[]{:S(2)}) async-start(f32[256,1,128]{2,1,0:T(1,128)} %get-tuple-element.67), calls=%async_computation.2 | async-start | bytes 262144 | tf_op jit(solution)/shard_map/all_to_all | solution.py:376
  83.8 2.1 %collective-permute-start.11 = (bf16[128,512]{1,0:T(8,128)(2,1)S(1)}, bf16[128,512]{1,0:T(8,128)(2,1)S(1)}, u32[]{:S(2)}, u32[]{:S(2)}) collective-permute-start(bf16[128,512]{1,0:T(8,128)(2,1)S(1)} %copy-done.6), channel_id=1, source_target_pairs={{0,128},{1,129},{2,130},{3,131},{4,132},{5,133},{6,134},{7,135},{8... | collective-permute-start | bytes 393224 | tf_op jit(solution)/shard_map/ppermute | solution.py:50
  85.9 3.0 %collective-permute-done.10.refs_1_ = bf16[128,512]{1,0:T(8,128)(2,1)S(1)} collective-permute-done((bf16[128,512]{1,0:T(8,128)(2,1)S(1)}, bf16[128,512]{1,0:T(8,128)(2,1)S(1)}, u32[]{:S(2)}, u32[]{:S(2)}) %collective-permute-start.10) | collective-permute-done | bytes 131104 | tf_op jit(solution)/shard_map/ppermute | solution.py:50
  88.9 1.7 collective-permute-done.11.refs_2_
  90.6 3.6 %collective-permute-done.12.refs_3_ = bf16[128,512]{1,0:T(8,128)(2,1)S(1)} collective-permute-done((bf16[128,512]{1,0:T(8,128)(2,1)S(1)}, bf16[128,512]{1,0:T(8,128)(2,1)S(1)}, u32[]{:S(2)}, u32[]{:S(2)}) %collective-permute-start.12) | collective-permute-done | bytes 131104 | tf_op jit(solution)/shard_map/ppermute | solution.py:50
  95.8 2.3 %fusion.12 = (bf16[256,256]{1,0:T(8,128)(2,1)}, f32[256,256]{1,0:T(8,128)}, f32[256,256]{1,0:T(8,128)}, f32[256,256]{1,0:T(8,128)}) fusion(f32[256,256]{1,0:T(8,128)} %param.18, f32[256,256]{1,0:T(8,128)S(1)} %get-tuple-element.66, f32[]{:T(128)S(6)} %min_shard_map.3, f32[256,256]{1,0:T(8,128)} %param.19, f32[256,256]{1,0:T(8,128)} %param.20), kind=kLoop, calls=%fused_computation.28 | loop fusion | flops 1114112 | bytes 1966084 | tf_op jit(solution)/shard_map/convert_element_type | solution.py:384
  98.1 1.4 collective-permute-start.18
  102.5 1.3 collective-permute-start.15
  105.6 1.7 collective-permute-start.17
  108.2 5.2 %collective-permute-done.20.w3 = bf16[256,256]{1,0:T(8,128)(2,1)} collective-permute-done((bf16[256,256]{1,0:T(8,128)(2,1)}, bf16[256,256]{1,0:T(8,128)(2,1)}, u32[]{:S(2)}, u32[]{:S(2)}) %collective-permute-start.20) | collective-permute-done | bytes 131104 | tf_op jit(solution)/shard_map/ppermute | solution.py:50
  113.4 5.8 %collective-permute-done.17.refs_8_ = bf16[256,512]{1,0:T(8,128)(2,1)} collective-permute-done((bf16[256,512]{1,0:T(8,128)(2,1)S(1)}, bf16[256,512]{1,0:T(8,128)(2,1)}, u32[]{:S(2)}, u32[]{:S(2)}) %collective-permute-start.17) | collective-permute-done | bytes 262176 | tf_op jit(solution)/shard_map/ppermute | solution.py:50
  121.9 2.0 %shard_map.185 = bf16[512,1024]{1,0:T(8,128)(2,1)S(1)} custom-call(s32[5]{0:T(128)S(1)} %stack.38.place_ref, s32[1]{0:T(128)S(6)} %sub.27.which_ref, bf16[128,512]{1,0:T(8,128)(2,1)S(1)} %copy-done.6, bf16[128,512]{1,0:T(8,128)(2,1)S(1)} %copy-done.8, bf16[128,512]{1,0:T(8,128)(2,1)S(1)} %copy-done.11, bf16[128,512]{1,0:T(8,128)(2,1)S(1)} %copy-done.14, ...), custom_call_target="tpu_custom_call" | custom-call | flops 268435456 | bytes 3145728 | tf_op jit(solution)/shard_map/pallas_call | solution.py:103
  124.5 3.1 %shard_map.186 = (bf16[4,128,256]{2,1,0:T(8,128)(2,1)S(1)}, bf16[4,128,256]{2,1,0:T(8,128)(2,1)}) custom-call(s32[5]{0:T(128)S(1)} %stack.38.place_ref, bf16[8,512,256]{2,1,0:T(8,128)(2,1)S(1)} %all-to-all-done.1.refs_0_.own_ref, bf16[8,512,256]{2,1,0:T(8,128)(2,1)} %collective-permute-done.13.other_ref, bf16[256,256]{1,0:T(8,128)(2,1)} %get-tuple-element.79.w0, ...), custom_call_target="tpu_custom_call" | custom-call | flops 536870912 | bytes 5242880 | tf_op jit(solution)/shard_map/pallas_call | solution.py:103
  133.5 2.0 %shard_map.187 = (bf16[128,1024]{1,0:T(8,128)(2,1)S(1)}, bf16[128,1024]{1,0:T(8,128)(2,1)S(1)}, bf16[128,1024]{1,0:T(8,128)(2,1)S(1)}, bf16[128,1024]{1,0:T(8,128)(2,1)S(1)}) custom-call(s32[5]{0:T(128)S(1)} %stack.38.place_ref, s32[1]{0:T(128)} %bitcast.5.which_ref, bf16[128,512]{1,0:T(8,128)(2,1)S(1)} %copy-done.6, bf16[128,512]{1,0:T(8,128)(2,1)S(1)} %copy-done.9, ...), custom_call_target="tpu_custom_call" | custom-call | flops 268435456 | bytes 4194304 | tf_op jit(solution)/shard_map/pallas_call | solution.py:103
  135.5 2.4 %collective-permute-start.26 = (bf16[128,1024]{1,0:T(8,128)(2,1)S(1)}, bf16[128,1024]{1,0:T(8,128)(2,1)S(1)}, u32[]{:S(2)}, u32[]{:S(2)}) collective-permute-start(bf16[128,1024]{1,0:T(8,128)(2,1)S(1)} %get-tuple-element.91), channel_id=1, source_target_pairs={{0,2},{1,3},{2,4},{3,5},{4,6},{5,7},{6,0},{7,1},{8,10},{9,11},{10,... | collective-permute-start | bytes 786440 | tf_op jit(solution)/shard_map/ppermute | solution.py:50
  137.9 3.5 %collective-permute-start.27 = (bf16[128,1024]{1,0:T(8,128)(2,1)S(1)}, bf16[128,1024]{1,0:T(8,128)(2,1)S(1)}, u32[]{:S(2)}, u32[]{:S(2)}) collective-permute-start(bf16[128,1024]{1,0:T(8,128)(2,1)S(1)} %get-tuple-element.92), channel_id=1, source_target_pairs={{0,4},{1,5},{2,6},{3,7},{4,0},{5,1},{6,2},{7,3},{8,12},{9,13},{10,... | collective-permute-start | bytes 786440 | tf_op jit(solution)/shard_map/ppermute | solution.py:50
  141.4 2.8 %collective-permute-start.28 = (bf16[128,1024]{1,0:T(8,128)(2,1)S(1)}, bf16[128,1024]{1,0:T(8,128)(2,1)S(1)}, u32[]{:S(2)}, u32[]{:S(2)}) collective-permute-start(bf16[128,1024]{1,0:T(8,128)(2,1)S(1)} %get-tuple-element.93), channel_id=1, source_target_pairs={{0,6},{1,7},{2,0},{3,1},{4,2},{5,3},{6,4},{7,5},{8,14},{9,15},{10,... | collective-permute-start | bytes 786440 | tf_op jit(solution)/shard_map/ppermute | solution.py:50
  146.0 1.2 collective-permute-start.24
  147.3 1.3 collective-permute-start.25
  148.5 1.4 multiply_subtract_fusion
  150.0 8.7 %collective-permute-done.27.refs_2_ = bf16[128,1024]{1,0:T(8,128)(2,1)S(1)} collective-permute-done((bf16[128,1024]{1,0:T(8,128)(2,1)S(1)}, bf16[128,1024]{1,0:T(8,128)(2,1)S(1)}, u32[]{:S(2)}, u32[]{:S(2)}) %collective-permute-start.27) | collective-permute-done | bytes 262176 | tf_op jit(solution)/shard_map/ppermute | solution.py:50
  158.7 7.2 %collective-permute-done.28.refs_3_ = bf16[128,1024]{1,0:T(8,128)(2,1)S(1)} collective-permute-done((bf16[128,1024]{1,0:T(8,128)(2,1)S(1)}, bf16[128,1024]{1,0:T(8,128)(2,1)S(1)}, u32[]{:S(2)}, u32[]{:S(2)}) %collective-permute-start.28) | collective-permute-done | bytes 262176 | tf_op jit(solution)/shard_map/ppermute | solution.py:50
  166.6 1.9 %collective-permute-start.29 = (bf16[128,1024]{1,0:T(8,128)(2,1)S(1)}, bf16[128,1024]{1,0:T(8,128)(2,1)S(1)}, u32[]{:S(2)}, u32[]{:S(2)}) collective-permute-start(bf16[128,1024]{1,0:T(8,128)(2,1)S(1)} %shard_map.188), channel_id=1, source_target_pairs={{0,0},{1,32},{2,64},{3,96},{4,128},{5,160},{6,192},{7,224},{8,8},{... | collective-permute-start | bytes 786440 | tf_op jit(solution)/shard_map/ppermute | solution.py:50
  169.3 19.0 %collective-permute-done.29 = bf16[128,1024]{1,0:T(8,128)(2,1)S(1)} collective-permute-done((bf16[128,1024]{1,0:T(8,128)(2,1)S(1)}, bf16[128,1024]{1,0:T(8,128)(2,1)S(1)}, u32[]{:S(2)}, u32[]{:S(2)}) %collective-permute-start.29) | collective-permute-done | bytes 262176 | tf_op jit(solution)/shard_map/ppermute | solution.py:50
  (105 shorter events, 25.4 us)
Async XLA Ops:
  5.4 5.8 %copy-start.25 = (bf16[128,256]{1,0:T(8,128)(2,1)S(1)}, bf16[128,256]{1,0:T(8,128)(2,1)}, u32[]{:S(2)}) copy-start(bf16[128,256]{1,0:T(8,128)(2,1)} %cot_ref.3) | copy-start | bytes 196612
  5.4 30.9 %all-to-all-start = ((bf16[8,128,1024]{2,1,0:T(8,128)(2,1)}), bf16[8,128,1024]{2,1,0:T(8,128)(2,1)S(1)}, u32[]{:S(2)}, u32[]{:S(2)}) async-start(bf16[8,128,1024]{2,1,0:T(8,128)(2,1)} %shard_map.179), calls=%async_computation | async-start | bytes 4194304 | tf_op jit(solution)/shard_map/all_to_all | solution.py:328
  12.8 20.8 %copy-start.5 = (bf16[128,8192]{1,0:T(8,128)(2,1)S(1)}, bf16[128,8192]{1,0:T(8,128)(2,1)}, u32[]{:S(2)}) copy-start(bf16[128,8192]{1,0:T(8,128)(2,1)} %refs_8_.1) | copy-start | bytes 6291460
  13.5 8.0 %collective-permute-start = (bf16[64,2560]{1,0:T(8,128)(2,1)S(1)}, bf16[64,2560]{1,0:T(8,128)(2,1)S(1)}, u32[]{:S(2)}, u32[]{:S(2)}) collective-permute-start(bf16[64,2560]{1,0:T(8,128)(2,1)S(1)} %get-tuple-element.53), channel_id=1, source_target_pairs={{0,64},{1,65},{2,66},{3,67},{4,68},{5,69},{6,70},{7,71},{8,72},{9,... | collective-permute-start | bytes 983048 | tf_op jit(solution)/shard_map/ppermute | solution.py:50
  13.7 11.7 %collective-permute-start.1 = (bf16[64,2560]{1,0:T(8,128)(2,1)S(1)}, bf16[64,2560]{1,0:T(8,128)(2,1)S(1)}, u32[]{:S(2)}, u32[]{:S(2)}) collective-permute-start(bf16[64,2560]{1,0:T(8,128)(2,1)S(1)} %get-tuple-element.54), channel_id=1, source_target_pairs={{0,128},{1,129},{2,130},{3,131},{4,132},{5,133},{6,134},{7,135},{8... | collective-permute-start | bytes 983048 | tf_op jit(solution)/shard_map/ppermute | solution.py:50
  15.9 16.0 %collective-permute-start.2 = (bf16[64,2560]{1,0:T(8,128)(2,1)S(1)}, bf16[64,2560]{1,0:T(8,128)(2,1)S(1)}, u32[]{:S(2)}, u32[]{:S(2)}) collective-permute-start(bf16[64,2560]{1,0:T(8,128)(2,1)S(1)} %get-tuple-element.55), channel_id=1, source_target_pairs={{0,192},{1,193},{2,194},{3,195},{4,196},{5,197},{6,198},{7,199},{8... | collective-permute-start | bytes 983048 | tf_op jit(solution)/shard_map/ppermute | solution.py:50
  21.5 10.9 %collective-permute-start.3 = (bf16[64,2560]{1,0:T(8,128)(2,1)S(1)}, bf16[64,2560]{1,0:T(8,128)(2,1)S(1)}, u32[]{:S(2)}, u32[]{:S(2)}) collective-permute-start(bf16[64,2560]{1,0:T(8,128)(2,1)S(1)} %collective-permute-done.refs_1_), channel_id=1, source_target_pairs={{0,1},{1,0},{2,3},{3,2},{4,5},{5,4},{6,7},{7,6},{8,9},{9,8},{10,11... | collective-permute-start | bytes 983048 | tf_op jit(solution)/shard_map/ppermute | solution.py:50
  25.4 7.0 %collective-permute-start.4 = (bf16[64,2560]{1,0:T(8,128)(2,1)S(1)}, bf16[64,2560]{1,0:T(8,128)(2,1)S(1)}, u32[]{:S(2)}, u32[]{:S(2)}) collective-permute-start(bf16[64,2560]{1,0:T(8,128)(2,1)S(1)} %collective-permute-done.1.refs_2_), channel_id=1, source_target_pairs={{0,1},{1,0},{2,3},{3,2},{4,5},{5,4},{6,7},{7,6},{8,9},{9,8},{10,11... | collective-permute-start | bytes 983048 | tf_op jit(solution)/shard_map/ppermute | solution.py:50
  31.9 1.8 collective-permute-start.5
  37.6 29.8 %all-to-all-start.1 = ((bf16[8,512,256]{2,1,0:T(8,128)(2,1)}), bf16[8,512,256]{2,1,0:T(8,128)(2,1)S(1)}, u32[]{:S(2)}, u32[]{:S(2)}) async-start(bf16[8,512,256]{2,1,0:T(8,128)(2,1)} %copy-done), calls=%async_computation.1 | async-start | bytes 4194304 | tf_op jit(solution)/shard_map/all_to_all | solution.py:328
  42.8 4.8 %copy-start.2 = (bf16[8,128,1024]{2,1,0:T(8,128)(2,1)S(1)}, bf16[8,128,1024]{2,1,0:T(8,128)(2,1)}, u32[]{:S(2)}) copy-start(bf16[8,128,1024]{2,1,0:T(8,128)(2,1)} %copy-done.1) | copy-start | bytes 6291460
  44.2 3.3 %collective-permute-start.6 = (bf16[8,128,512]{2,1,0:T(8,128)(2,1)S(1)}, bf16[8,128,512]{2,1,0:T(8,128)(2,1)S(1)}, u32[]{:S(2)}, u32[]{:S(2)}) collective-permute-start(bf16[8,128,512]{2,1,0:T(8,128)(2,1)S(1)} %slice.26), channel_id=1, source_target_pairs={{0,1},{1,0},{2,3},{3,2},{4,5},{5,4},{6,7},{7,6},{8,9},{9,8},{10,11... | collective-permute-start | bytes 3145736 | tf_op jit(solution)/shard_map/ppermute | solution.py:50
  48.8 34.7 %copy-start.6 = (bf16[128,512]{1,0:T(8,128)(2,1)S(1)}, bf16[128,512]{1,0:T(8,128)(2,1)}, u32[]{:S(2)}) copy-start(bf16[128,512]{1,0:T(8,128)(2,1)} %refs_0_.1) | copy-start | bytes 393220
  48.8 7.6 %collective-permute-start.7 = (bf16[512,256]{1,0:T(8,128)(2,1)S(1)}, bf16[512,256]{1,0:T(8,128)(2,1)S(1)}, u32[]{:S(2)}, u32[]{:S(2)}) collective-permute-start(bf16[512,256]{1,0:T(8,128)(2,1)S(1)} %get-tuple-element.60), channel_id=1, source_target_pairs={{0,64},{1,65},{2,66},{3,67},{4,68},{5,69},{6,70},{7,71},{8,72},{9,... | collective-permute-start | bytes 786440 | tf_op jit(solution)/shard_map/ppermute | solution.py:50
  50.1 8.7 %collective-permute-start.8 = (bf16[512,256]{1,0:T(8,128)(2,1)S(1)}, bf16[512,256]{1,0:T(8,128)(2,1)S(1)}, u32[]{:S(2)}, u32[]{:S(2)}) collective-permute-start(bf16[512,256]{1,0:T(8,128)(2,1)S(1)} %get-tuple-element.61), channel_id=1, source_target_pairs={{0,128},{1,129},{2,130},{3,131},{4,132},{5,133},{6,134},{7,135},{8... | collective-permute-start | bytes 786440 | tf_op jit(solution)/shard_map/ppermute | solution.py:50
  51.4 14.0 %collective-permute-start.9 = (bf16[512,256]{1,0:T(8,128)(2,1)S(1)}, bf16[512,256]{1,0:T(8,128)(2,1)S(1)}, u32[]{:S(2)}, u32[]{:S(2)}) collective-permute-start(bf16[512,256]{1,0:T(8,128)(2,1)S(1)} %get-tuple-element.62), channel_id=1, source_target_pairs={{0,192},{1,193},{2,194},{3,195},{4,196},{5,197},{6,198},{7,199},{8... | collective-permute-start | bytes 786440 | tf_op jit(solution)/shard_map/ppermute | solution.py:50
  67.5 26.8 %collective-permute-start.13 = (bf16[8,512,256]{2,1,0:T(8,128)(2,1)S(1)}, bf16[8,512,256]{2,1,0:T(8,128)(2,1)}, u32[]{:S(2)}, u32[]{:S(2)}) collective-permute-start(bf16[8,512,256]{2,1,0:T(8,128)(2,1)S(1)} %all-to-all-done.1.refs_0_.own_ref), channel_id=1, source_target_pairs={{0,1},{1,0},{2,3},{3,2},{4,5},{5,4},{6,7},{7,6},{8,9},{9,8},{10,11... | collective-permute-start | bytes 6291464 | tf_op jit(solution)/shard_map/ppermute | solution.py:50
  70.5 23.7 %all-to-all-start.2 = ((f32[256,1,128]{2,1,0:T(1,128)}), f32[256,1,128]{2,1,0:T(1,128)S(1)}, u32[]{:S(2)}, u32[]{:S(2)}) async-start(f32[256,1,128]{2,1,0:T(1,128)} %get-tuple-element.67), calls=%async_computation.2 | async-start | bytes 262144 | tf_op jit(solution)/shard_map/all_to_all | solution.py:376
  83.5 5.5 %collective-permute-start.10 = (bf16[128,512]{1,0:T(8,128)(2,1)S(1)}, bf16[128,512]{1,0:T(8,128)(2,1)S(1)}, u32[]{:S(2)}, u32[]{:S(2)}) collective-permute-start(bf16[128,512]{1,0:T(8,128)(2,1)S(1)} %copy-done.6), channel_id=1, source_target_pairs={{0,64},{1,65},{2,66},{3,67},{4,68},{5,69},{6,70},{7,71},{8,72},{9,... | collective-permute-start | bytes 393224 | tf_op jit(solution)/shard_map/ppermute | solution.py:50
  83.8 6.8 %collective-permute-start.11 = (bf16[128,512]{1,0:T(8,128)(2,1)S(1)}, bf16[128,512]{1,0:T(8,128)(2,1)S(1)}, u32[]{:S(2)}, u32[]{:S(2)}) collective-permute-start(bf16[128,512]{1,0:T(8,128)(2,1)S(1)} %copy-done.6), channel_id=1, source_target_pairs={{0,128},{1,129},{2,130},{3,131},{4,132},{5,133},{6,134},{7,135},{8... | collective-permute-start | bytes 393224 | tf_op jit(solution)/shard_map/ppermute | solution.py:50
  85.9 8.3 %collective-permute-start.12 = (bf16[128,512]{1,0:T(8,128)(2,1)S(1)}, bf16[128,512]{1,0:T(8,128)(2,1)S(1)}, u32[]{:S(2)}, u32[]{:S(2)}) collective-permute-start(bf16[128,512]{1,0:T(8,128)(2,1)S(1)} %copy-done.6), channel_id=1, source_target_pairs={{0,192},{1,193},{2,194},{3,195},{4,196},{5,197},{6,198},{7,199},{8... | collective-permute-start | bytes 393224 | tf_op jit(solution)/shard_map/ppermute | solution.py:50
  88.9 13.1 %copy-start.7 = (bf16[128,512]{1,0:T(8,128)(2,1)}, bf16[128,512]{1,0:T(8,128)(2,1)S(1)}, u32[]{:S(2)}) copy-start(bf16[128,512]{1,0:T(8,128)(2,1)S(1)} %collective-permute-done.10.refs_1_) | copy-start | bytes 393220
  90.6 11.4 %copy-start.10 = (bf16[128,512]{1,0:T(8,128)(2,1)}, bf16[128,512]{1,0:T(8,128)(2,1)S(1)}, u32[]{:S(2)}) copy-start(bf16[128,512]{1,0:T(8,128)(2,1)S(1)} %collective-permute-done.11.refs_2_) | copy-start | bytes 393220
  94.2 5.7 %copy-start.13 = (bf16[128,512]{1,0:T(8,128)(2,1)}, bf16[128,512]{1,0:T(8,128)(2,1)S(1)}, u32[]{:S(2)}) copy-start(bf16[128,512]{1,0:T(8,128)(2,1)S(1)} %collective-permute-done.12.refs_3_) | copy-start | bytes 393220
  95.8 6.2 %copy-start.26 = (f32[256,512]{1,0:T(8,128)S(1)}, f32[256,512]{1,0:T(8,128)}, u32[]{:S(2)}) copy-start(f32[256,512]{1,0:T(8,128)} %param.21) | copy-start | bytes 1572868
  95.8 6.2 %copy-start.28 = (f32[256,512]{1,0:T(8,128)S(1)}, f32[256,512]{1,0:T(8,128)}, u32[]{:S(2)}) copy-start(f32[256,512]{1,0:T(8,128)} %param.22) | copy-start | bytes 1572868
  95.8 6.2 %copy-start.30 = (f32[256,512]{1,0:T(8,128)S(1)}, f32[256,512]{1,0:T(8,128)}, u32[]{:S(2)}) copy-start(f32[256,512]{1,0:T(8,128)} %param.23) | copy-start | bytes 1572868
  98.1 6.8 %collective-permute-start.18 = (bf16[256,256]{1,0:T(8,128)(2,1)}, bf16[256,256]{1,0:T(8,128)(2,1)S(1)}, u32[]{:S(2)}, u32[]{:S(2)}) collective-permute-start(bf16[256,256]{1,0:T(8,128)(2,1)} %get-tuple-element.79.w0), channel_id=1, source_target_pairs={{0,64},{1,65},{2,66},{3,67},{4,68},{5,69},{6,70},{7,71},{8,72},{9,... | collective-permute-start | bytes 393224 | tf_op jit(solution)/shard_map/ppermute | solution.py:50
  99.5 7.7 %collective-permute-start.19 = (bf16[256,256]{1,0:T(8,128)(2,1)}, bf16[256,256]{1,0:T(8,128)(2,1)S(1)}, u32[]{:S(2)}, u32[]{:S(2)}) collective-permute-start(bf16[256,256]{1,0:T(8,128)(2,1)} %get-tuple-element.79.w0), channel_id=1, source_target_pairs={{0,128},{1,129},{2,130},{3,131},{4,132},{5,133},{6,134},{7,135},{8... | collective-permute-start | bytes 393224 | tf_op jit(solution)/shard_map/ppermute | solution.py:50
  100.8 18.4 %collective-permute-start.14 = (bf16[4,128,512]{2,1,0:T(8,128)(2,1)}, bf16[4,128,512]{2,1,0:T(8,128)(2,1)S(1)}, u32[]{:S(2)}, u32[]{:S(2)}) collective-permute-start(bf16[4,128,512]{2,1,0:T(8,128)(2,1)} %pad_maximum_fusion), channel_id=1, source_target_pairs={{0,32},{1,33},{2,34},{3,35},{4,36},{5,37},{6,38},{7,39},{8,40},{9,... | collective-permute-start | bytes 1572872 | tf_op jit(solution)/shard_map/ppermute | solution.py:50
  102.5 10.9 %collective-permute-start.15 = (bf16[256,512]{1,0:T(8,128)(2,1)S(1)}, bf16[256,512]{1,0:T(8,128)(2,1)}, u32[]{:S(2)}, u32[]{:S(2)}) collective-permute-start(bf16[256,512]{1,0:T(8,128)(2,1)S(1)} %subtract_convert_fusion.refs_5_), channel_id=1, source_target_pairs={{0,8},{1,9},{2,10},{3,11},{4,12},{5,13},{6,14},{7,15},{8,16},{9,17... | collective-permute-start | bytes 786440 | tf_op jit(solution)/shard_map/ppermute | solution.py:50
  103.8 9.5 %collective-permute-start.16 = (bf16[256,512]{1,0:T(8,128)(2,1)S(1)}, bf16[256,512]{1,0:T(8,128)(2,1)}, u32[]{:S(2)}, u32[]{:S(2)}) collective-permute-start(bf16[256,512]{1,0:T(8,128)(2,1)S(1)} %subtract_convert_fusion.refs_5_), channel_id=1, source_target_pairs={{0,16},{1,17},{2,18},{3,19},{4,20},{5,21},{6,22},{7,23},{8,24},{9,... | collective-permute-start | bytes 786440 | tf_op jit(solution)/shard_map/ppermute | solution.py:50
  105.6 13.6 %collective-permute-start.17 = (bf16[256,512]{1,0:T(8,128)(2,1)S(1)}, bf16[256,512]{1,0:T(8,128)(2,1)}, u32[]{:S(2)}, u32[]{:S(2)}) collective-permute-start(bf16[256,512]{1,0:T(8,128)(2,1)S(1)} %subtract_convert_fusion.refs_5_), channel_id=1, source_target_pairs={{0,24},{1,25},{2,26},{3,27},{4,28},{5,29},{6,30},{7,31},{8,0},{9,1... | collective-permute-start | bytes 786440 | tf_op jit(solution)/shard_map/ppermute | solution.py:50
  107.9 5.5 %collective-permute-start.20 = (bf16[256,256]{1,0:T(8,128)(2,1)}, bf16[256,256]{1,0:T(8,128)(2,1)}, u32[]{:S(2)}, u32[]{:S(2)}) collective-permute-start(bf16[256,256]{1,0:T(8,128)(2,1)} %get-tuple-element.79.w0), channel_id=1, source_target_pairs={{0,192},{1,193},{2,194},{3,195},{4,196},{5,197},{6,198},{7,199},{8... | collective-permute-start | bytes 393224 | tf_op jit(solution)/shard_map/ppermute | solution.py:50
  121.9 2.6 %copy-start.24 = (bf16[256,256]{1,0:T(8,128)(2,1)S(1)}, bf16[256,256]{1,0:T(8,128)(2,1)}, u32[]{:S(2)}) copy-start(bf16[256,256]{1,0:T(8,128)(2,1)} %copy-done.23) | copy-start | bytes 393220
  123.9 4.5 %collective-permute-start.21 = (bf16[512,1024]{1,0:T(8,128)(2,1)S(1)}, bf16[512,1024]{1,0:T(8,128)(2,1)S(1)}, u32[]{:S(2)}, u32[]{:S(2)}) collective-permute-start(bf16[512,1024]{1,0:T(8,128)(2,1)S(1)} %shard_map.185), channel_id=1, source_target_pairs={{0,1},{1,0},{2,3},{3,2},{4,5},{5,4},{6,7},{7,6},{8,9},{9,8},{10,11... | collective-permute-start | bytes 3145736 | tf_op jit(solution)/shard_map/ppermute | solution.py:50
  129.3 14.9 %collective-permute-start.22 = (bf16[4,128,256]{2,1,0:T(8,128)(2,1)}, bf16[4,128,256]{2,1,0:T(8,128)(2,1)}, u32[]{:S(2)}, u32[]{:S(2)}) collective-permute-start(bf16[4,128,256]{2,1,0:T(8,128)(2,1)} %get-tuple-element.90), channel_id=1, source_target_pairs={{0,32},{1,33},{2,34},{3,35},{4,36},{5,37},{6,38},{7,39},{8,40},{9,... | collective-permute-start | bytes 786440 | tf_op jit(solution)/shard_map/ppermute | solution.py:50
  133.5 10.8 %copy-start.19 = (bf16[4,128,256]{2,1,0:T(8,128)(2,1)S(1)}, bf16[4,128,256]{2,1,0:T(8,128)(2,1)}, u32[]{:S(2)}) copy-start(bf16[4,128,256]{2,1,0:T(8,128)(2,1)} %copy-done.18) | copy-start | bytes 786436
  133.5 15.1 %copy-start.27 = (f32[256,512]{1,0:T(8,128)S(1)}, f32[256,512]{1,0:T(8,128)}, u32[]{:S(2)}) copy-start(f32[256,512]{1,0:T(8,128)} %param.21) | copy-start | bytes 1572868
  133.5 15.1 %copy-start.29 = (f32[256,512]{1,0:T(8,128)S(1)}, f32[256,512]{1,0:T(8,128)}, u32[]{:S(2)}) copy-start(f32[256,512]{1,0:T(8,128)} %param.22) | copy-start | bytes 1572868
  133.5 15.1 %copy-start.31 = (f32[256,512]{1,0:T(8,128)S(1)}, f32[256,512]{1,0:T(8,128)}, u32[]{:S(2)}) copy-start(f32[256,512]{1,0:T(8,128)} %param.23) | copy-start | bytes 1572868
  135.5 11.7 %collective-permute-start.26 = (bf16[128,1024]{1,0:T(8,128)(2,1)S(1)}, bf16[128,1024]{1,0:T(8,128)(2,1)S(1)}, u32[]{:S(2)}, u32[]{:S(2)}) collective-permute-start(bf16[128,1024]{1,0:T(8,128)(2,1)S(1)} %get-tuple-element.91), channel_id=1, source_target_pairs={{0,2},{1,3},{2,4},{3,5},{4,6},{5,7},{6,0},{7,1},{8,10},{9,11},{10,... | collective-permute-start | bytes 786440 | tf_op jit(solution)/shard_map/ppermute | solution.py:50
  137.9 20.8 %collective-permute-start.27 = (bf16[128,1024]{1,0:T(8,128)(2,1)S(1)}, bf16[128,1024]{1,0:T(8,128)(2,1)S(1)}, u32[]{:S(2)}, u32[]{:S(2)}) collective-permute-start(bf16[128,1024]{1,0:T(8,128)(2,1)S(1)} %get-tuple-element.92), channel_id=1, source_target_pairs={{0,4},{1,5},{2,6},{3,7},{4,0},{5,1},{6,2},{7,3},{8,12},{9,13},{10,... | collective-permute-start | bytes 786440 | tf_op jit(solution)/shard_map/ppermute | solution.py:50
  141.4 24.5 %collective-permute-start.28 = (bf16[128,1024]{1,0:T(8,128)(2,1)S(1)}, bf16[128,1024]{1,0:T(8,128)(2,1)S(1)}, u32[]{:S(2)}, u32[]{:S(2)}) collective-permute-start(bf16[128,1024]{1,0:T(8,128)(2,1)S(1)} %get-tuple-element.93), channel_id=1, source_target_pairs={{0,6},{1,7},{2,0},{3,1},{4,2},{5,3},{6,4},{7,5},{8,14},{9,15},{10,... | collective-permute-start | bytes 786440 | tf_op jit(solution)/shard_map/ppermute | solution.py:50
  145.3 23.2 %collective-permute-start.23 = (bf16[128,256]{1,0:T(8,128)(2,1)S(1)}, bf16[128,256]{1,0:T(8,128)(2,1)S(1)}, u32[]{:S(2)}, u32[]{:S(2)}) collective-permute-start(bf16[128,256]{1,0:T(8,128)(2,1)S(1)} %get-tuple-element.101), channel_id=1, source_target_pairs={{0,8},{1,9},{2,10},{3,11},{4,12},{5,13},{6,14},{7,15},{8,16},{9,17... | collective-permute-start | bytes 196616 | tf_op jit(solution)/shard_map/ppermute | solution.py:50
  146.0 22.5 %collective-permute-start.24 = (bf16[128,256]{1,0:T(8,128)(2,1)S(1)}, bf16[128,256]{1,0:T(8,128)(2,1)S(1)}, u32[]{:S(2)}, u32[]{:S(2)}) collective-permute-start(bf16[128,256]{1,0:T(8,128)(2,1)S(1)} %get-tuple-element.103), channel_id=1, source_target_pairs={{0,16},{1,17},{2,18},{3,19},{4,20},{5,21},{6,22},{7,23},{8,24},{9,... | collective-permute-start | bytes 196616 | tf_op jit(solution)/shard_map/ppermute | solution.py:50
  147.3 21.3 %collective-permute-start.25 = (bf16[128,256]{1,0:T(8,128)(2,1)S(1)}, bf16[128,256]{1,0:T(8,128)(2,1)S(1)}, u32[]{:S(2)}, u32[]{:S(2)}) collective-permute-start(bf16[128,256]{1,0:T(8,128)(2,1)S(1)} %get-tuple-element.102), channel_id=1, source_target_pairs={{0,24},{1,25},{2,26},{3,27},{4,28},{5,29},{6,30},{7,31},{8,0},{9,1... | collective-permute-start | bytes 196616 | tf_op jit(solution)/shard_map/ppermute | solution.py:50
  166.6 21.6 %collective-permute-start.29 = (bf16[128,1024]{1,0:T(8,128)(2,1)S(1)}, bf16[128,1024]{1,0:T(8,128)(2,1)S(1)}, u32[]{:S(2)}, u32[]{:S(2)}) collective-permute-start(bf16[128,1024]{1,0:T(8,128)(2,1)S(1)} %shard_map.188), channel_id=1, source_target_pairs={{0,0},{1,32},{2,64},{3,96},{4,128},{5,160},{6,192},{7,224},{8,8},{... | collective-permute-start | bytes 786440 | tf_op jit(solution)/shard_map/ppermute | solution.py:50
  (17 other events, 19.0 us)
